TPU v7x, 128 devices: a whole 4x4x4 slice. The times are simulated.
128 devices in a mesh: group: 16 (over x, y_hi, core), tensor: 8 (over y_lo, z).
Axes of the slice: x: 4, y: 4 (y_hi: 2, y_lo: 2; y = y_hi * 2 + y_lo), z: 4, core: 2. Of those that a mesh axis runs over, the one named last changes fastest.
Arguments:
- completion_query_slots: bfloat16 [8192, 8192], P('group', 'tensor'), may hold values from -8 to 8
- completion_key_array: bfloat16 [8192, 1024], P('group', 'tensor'), may hold values from -6 to 6
- completion_value_array: bfloat16 [8192, 1024], P('group', 'tensor'), may hold values from -6 to 6
- comp_dout: bfloat16 [8192, 8192], P('group', 'tensor'), may hold values from -192 to 192
- prompt_query_array: bfloat16 [1536, 8192], P('group', 'tensor'), may hold values from -8 to 8
- prompt_key_array: bfloat16 [1536, 1024], P('group', 'tensor'), may hold values from -8 to 8
- prompt_value_array: bfloat16 [1536, 1024], P('group', 'tensor'), may hold values from -6 to 6
- prompt_output_cotangent: bfloat16 [1536, 8192], P('group', 'tensor'), may hold values from -48 to 48
- lengths: int32 [16], replicated, may hold values from 1 to 4, 40 in all
- slot_of: int32 [16], replicated, may hold values from 0 to 15, each once
- passes: int32 [16, 32], P('group', 'tensor'), may hold values from 0 to 1
Outputs:
- comp_dq: bfloat16 [8192, 8192], P('group', 'tensor')
- completion_key_gradients: bfloat16 [8192, 1024], P('group', 'tensor')
- completion_value_gradients: bfloat16 [8192, 1024], P('group', 'tensor')
- prompt_dq: bfloat16 [1536, 8192], P('group', 'tensor')
- prompt_key_gradients: bfloat16 [1536, 1024], P('group', 'tensor')
- prompt_value_gradients: bfloat16 [1536, 1024], P('group', 'tensor')
Inputs may be any that keep to these rules, and one draw needn't show every extreme that they name: `lengths`: counts in blocks of 128 tokens; they sum to 40 and the longest completion has exactly 4 blocks. `slot_of`: each slot holds exactly one completion.
All inputs are finite; a program needn't handle non-finite values.
Results may differ from a plain program's by a relative error of at most 0.008.
Values may be sent and summed in bfloat16 or wider, within the bound.
A program may use at most 64 MiB of HBM per device.

v0:
```python
import jax
import jax.numpy as jnp
from jax import lax
from jax.sharding import PartitionSpec as P

HEAD_SIZE = 128
BLK = 128
MAXB = 4
TESTS = 32


MASKED = -1e30


def visible_mask(row_ids, key_ids, comp_rows, prompt_len, live_rows, prompt_base):
    is_comp = row_ids[:, None] < comp_rows
    key_prompt = key_ids[None, :] < prompt_len
    own_key = key_ids[None, :] - prompt_len
    comp_ok = key_prompt | (own_key <= row_ids[:, None]) & (own_key < live_rows)
    prompt_pos = prompt_base + row_ids[:, None] - comp_rows
    prompt_ok = key_prompt & (key_ids[None, :] <= prompt_pos)
    return jnp.where(is_comp, comp_ok, prompt_ok)


def per_device(
    completion_query_slots,
    completion_key_array,
    completion_value_array,
    comp_dout,
    prompt_query_array,
    prompt_key_array,
    prompt_value_array,
    prompt_output_cotangent,
    lengths,
    slot_of,
    passes,
):
    group_id = lax.axis_index("group")
    n_group = lax.axis_size("group")
    comp_rows = completion_query_slots.shape[0]
    prompt_rows = prompt_query_array.shape[0]
    kv_cols = completion_key_array.shape[1]
    heads_kv = kv_cols // HEAD_SIZE
    heads_q = completion_query_slots.shape[1] // HEAD_SIZE
    per_kv = heads_q // heads_kv
    prompt_len = prompt_rows * n_group
    score_scale = HEAD_SIZE ** (-0.5)
    slot_ids = jnp.arange(n_group, dtype=jnp.int32)
    local_count = jnp.sum(passes).astype(jnp.float32)
    own_count = lax.psum(local_count, "tensor")
    table = jnp.where(slot_ids == group_id, own_count / TESTS, 0.0)
    rewards = lax.psum(table, "group")
    center = jnp.mean(rewards)
    advantage = rewards - center
    own_advantage = jnp.sum(jnp.where(slot_ids == group_id, advantage, 0.0))
    own_blocks = jnp.sum(jnp.where(slot_of == group_id, lengths, 0))
    live_rows = own_blocks * BLK
    factor = own_advantage * MAXB / own_blocks.astype(jnp.float32)
    keep = (jnp.arange(comp_rows, dtype=jnp.int32) < live_rows).astype(jnp.float32)
    completion_cotangent = (comp_dout.astype(jnp.float32) * (factor * keep)[:, None]).astype(
        jnp.bfloat16
    )
    all_rows = comp_rows + prompt_rows
    queries = jnp.concatenate([completion_query_slots, prompt_query_array], axis=0).reshape(
        all_rows, heads_kv, per_kv, HEAD_SIZE
    )
    cots = jnp.concatenate([completion_cotangent, prompt_output_cotangent], axis=0).reshape(
        all_rows, heads_kv, per_kv, HEAD_SIZE
    )
    gathered_keys, gathered_values = (
        lax.all_gather(prompt_key_array, "group", axis=0, tiled=True),
        lax.all_gather(prompt_value_array, "group", axis=0, tiled=True),
    )
    key_rows = jnp.concatenate([gathered_keys, completion_key_array], axis=0).reshape(
        -1, heads_kv, HEAD_SIZE
    )
    value_rows = jnp.concatenate([gathered_values, completion_value_array], axis=0).reshape(
        -1, heads_kv, HEAD_SIZE
    )
    key_count = key_rows.shape[0]
    row_ids = jnp.arange(all_rows, dtype=jnp.int32)
    key_ids = jnp.arange(key_count, dtype=jnp.int32)
    prompt_base = group_id * prompt_rows
    visible = visible_mask(row_ids, key_ids, comp_rows, prompt_len, live_rows, prompt_base)

    def head_terms(head):
        query_head = lax.dynamic_index_in_dim(queries, head, 2, keepdims=False)
        cot_head = lax.dynamic_index_in_dim(cots, head, 2, keepdims=False)
        raw = (
            jnp.einsum("rhd,khd->rhk", query_head, key_rows, preferred_element_type=jnp.float32)
            * score_scale
        )
        scores = jnp.where(visible[:, None, :], raw, MASKED)
        row_top = jnp.max(scores, axis=2, keepdims=True)
        exps = jnp.exp(scores - row_top)
        row_total = jnp.sum(exps, axis=2, keepdims=True)
        weights = exps / row_total
        dweights = jnp.einsum(
            "rhd,khd->rhk", cot_head, value_rows, preferred_element_type=jnp.float32
        )
        drift = jnp.sum(weights * dweights, axis=2, keepdims=True)
        dscores = (weights * (dweights - drift)).astype(jnp.bfloat16)
        weights_b = weights.astype(jnp.bfloat16)
        head_dq = (
            jnp.einsum("rhk,khd->rhd", dscores, key_rows, preferred_element_type=jnp.float32)
            * score_scale
        )
        key_term = (
            jnp.einsum("rhk,rhd->khd", dscores, query_head, preferred_element_type=jnp.float32)
            * score_scale
        )
        value_term = jnp.einsum(
            "rhk,rhd->khd", weights_b, cot_head, preferred_element_type=jnp.float32
        )
        return (head_dq, key_term, value_term, row_top[..., 0], row_total[..., 0], drift[..., 0])

    query_zero = jnp.zeros((all_rows, heads_kv, per_kv, HEAD_SIZE), jnp.float32)

    def whole_step(head, state):
        query_grad, key_sum, value_sum = state
        head_dq, key_term, value_term, row_top, row_total, drift = head_terms(head)
        query_grad = lax.dynamic_update_index_in_dim(query_grad, head_dq, head, 2)
        return (query_grad, key_sum + key_term, value_sum + value_term)

    key_zero = jnp.zeros((key_count, heads_kv, HEAD_SIZE), jnp.float32)
    query_grad, key_sum, value_sum = lax.fori_loop(
        0, per_kv, whole_step, (query_zero, key_zero, key_zero)
    )
    key_grads = jnp.concatenate(
        [key_sum.reshape(key_count, kv_cols), value_sum.reshape(key_count, kv_cols)], axis=1
    )
    prompt_part = lax.psum_scatter(key_grads[:prompt_len], "group", scatter_dimension=0, tiled=True)
    comp_part = key_grads[prompt_len:]
    query_flat = query_grad.reshape(all_rows, heads_q * HEAD_SIZE)
    comp_dq = query_flat[:comp_rows].astype(jnp.bfloat16)
    prompt_dq = query_flat[comp_rows:].astype(jnp.bfloat16)
    completion_key_gradients = comp_part[:, :kv_cols].astype(jnp.bfloat16)
    completion_value_gradients = comp_part[:, kv_cols:].astype(jnp.bfloat16)
    prompt_key_gradients = prompt_part[:, :kv_cols].astype(jnp.bfloat16)
    prompt_value_gradients = prompt_part[:, kv_cols:].astype(jnp.bfloat16)
    return (
        comp_dq,
        completion_key_gradients,
        completion_value_gradients,
        prompt_dq,
        prompt_key_gradients,
        prompt_value_gradients,
    )


def solution(mesh):
    return jax.shard_map(
        per_device,
        mesh=mesh,
        in_specs=(
            P("group", "tensor"),
            P("group", "tensor"),
            P("group", "tensor"),
            P("group", "tensor"),
            P("group", "tensor"),
            P("group", "tensor"),
            P("group", "tensor"),
            P("group", "tensor"),
            P(),
            P(),
            P("group", "tensor"),
        ),
        out_specs=(
            P("group", "tensor"),
            P("group", "tensor"),
            P("group", "tensor"),
            P("group", "tensor"),
            P("group", "tensor"),
            P("group", "tensor"),
        ),
        check_vma=False,
    )
```

profile of v0, /device:TPU:1, one launch (start us, length us, event | category | flops | bytes accessed | tf_op | source)
XLA Modules:
  0.0 328.6 jit_solution(3789378443559651165)
XLA Ops:
  9.8 18.6 %psum.14 = f32[]{:T(128)} all-reduce(f32[]{:T(128)S(6)} %convert_element_type.46), channel_id=1, replica_groups=mesh['group'=16,'tensor'=8] {'tensor'}, use_global_device_ids=true, to_apply=%region_2.3 | all-reduce | flops 1 | bytes 8 | tf_op jit(solution)/shard_map/psum | solution.py:50
  29.0 37.0 %psum.15 = f32[16]{0:T(128)S(1)} all-reduce(f32[16]{0:T(128)S(1)} %compare_select_fusion.2), channel_id=1, replica_groups=mesh['group'=16,'tensor'=8] {'group'}, use_global_device_ids=true, to_apply=%region_3.4 | all-reduce | flops 16 | bytes 128 | tf_op jit(solution)/shard_map/psum | solution.py:52
  76.3 21.3 %all_gather.6 = bf16[1536,128]{1,0:T(8,128)(2,1)S(1)} all-gather(bf16[96,128]{1,0:T(8,128)(2,1)S(1)} %copy-done.10), channel_id=1, replica_groups=mesh['group'=16,'tensor'=8] {'group'}, dimensions={0}, use_global_device_ids=true | all-gather | bytes 417792 | tf_op jit(solution)/shard_map/all_gather | solution.py:71
  97.6 23.5 %all_gather.7 = bf16[1536,128]{1,0:T(8,128)(2,1)S(1)} all-gather(bf16[96,128]{1,0:T(8,128)(2,1)S(1)} %copy-done.11), channel_id=1, replica_groups=mesh['group'=16,'tensor'=8] {'group'}, dimensions={0}, use_global_device_ids=true | all-gather | bytes 417792 | tf_op jit(solution)/shard_map/all_gather | solution.py:72
  122.8 134.5 %while.18 = (s32[]{:T(128)}, bf16[608,1,8,128]{3,0,2,1:T(8,128)(2,1)}, f32[2048,1,128]{0,2,1:T(8,128)S(1)}, f32[2048,1,128]{0,2,1:T(8,128)}, bf16[608,1,8,128]{3...) while((s32[]{:T(128)}, ...), condition=%wide.region_10.11_spmd.clone, body=%wide.region_6.10_spmd.clone.sunk | while | flops 1623861504 | bytes 93148216 | solution.py:126
  122.8 3.6 %fusion.71 = (f32[608]{0:T(1024)S(1)}, f32[608,1,2048]{2,0,1:T(8,128)S(1)}) fusion(bf16[2048,1,128]{2,0,1:T(8,128)(2,1)} %get-tuple-element.383, bf16[608,1,8,128]{3,0,2,1:T(8,128)(2,1)S(1)} %get-tuple-element.382, s32[]{:T(128)} %get-tuple-element.363, s32[608]{0:T(1024)S(1)} %get-tuple-element.388, pred[2048]{0:T(1024)(128)(4,1)} %get-tuple-element.387, ...), kind=kOutput, calls=%fused_computation.69.clone.1 | convolution fusion | flops 329973152 | bytes 5680100 | tf_op jit(solution)/shard_map/while/body/eval_jaxpr/rhd,khd->rhk/dot_general | solution.py:90
  126.4 2.2 copy-done
  129.4 4.7 %fusion.77 = f32[2048,1,128]{0,2,1:T(8,128)} fusion(f32[2048,1,128]{0,2,1:T(8,128)} %get-tuple-element.366, pred[]{:T(512)S(6)} %compare.3, bf16[608,1,8,128]{3,0,2,1:T(8,128)(2,1)S(1)} %get-tuple-element.384, s32[]{:T(128)} %get-tuple-element.363, f32[608,1,2048]{2,0,1:T(8,128)} %copy-done, f32[608]{0:T(1024)S(1)} %fusion.72, ...), kind=kOutput, calls=%fused_computation.25.clone.1 | convolution fusion | flops 323026944 | bytes 7241733 | tf_op jit(solution)/shard_map/while/body/eval_jaxpr/rhk,rhd->khd/dot_general | solution.py:112
  139.3 3.6 %fusion.71 = (f32[608]{0:T(1024)S(1)}, f32[608,1,2048]{2,0,1:T(8,128)S(1)}) fusion(bf16[2048,1,128]{2,0,1:T(8,128)(2,1)} %get-tuple-element.383, bf16[608,1,8,128]{3,0,2,1:T(8,128)(2,1)S(1)} %get-tuple-element.382, s32[]{:T(128)} %get-tuple-element.363, s32[608]{0:T(1024)S(1)} %get-tuple-element.388, pred[2048]{0:T(1024)(128)(4,1)} %get-tuple-element.387, ...), kind=kOutput, calls=%fused_computation.69.clone.1 | convolution fusion | flops 329973152 | bytes 5680100 | tf_op jit(solution)/shard_map/while/body/eval_jaxpr/rhd,khd->rhk/dot_general | solution.py:90
  143.0 2.2 copy-done
  146.0 5.0 %fusion.77 = f32[2048,1,128]{0,2,1:T(8,128)} fusion(f32[2048,1,128]{0,2,1:T(8,128)} %get-tuple-element.366, pred[]{:T(512)S(6)} %compare.3, bf16[608,1,8,128]{3,0,2,1:T(8,128)(2,1)S(1)} %get-tuple-element.384, s32[]{:T(128)} %get-tuple-element.363, f32[608,1,2048]{2,0,1:T(8,128)} %copy-done, f32[608]{0:T(1024)S(1)} %fusion.72, ...), kind=kOutput, calls=%fused_computation.25.clone.1 | convolution fusion | flops 323026944 | bytes 7241733 | tf_op jit(solution)/shard_map/while/body/eval_jaxpr/rhk,rhd->khd/dot_general | solution.py:112
  156.1 3.6 %fusion.71 = (f32[608]{0:T(1024)S(1)}, f32[608,1,2048]{2,0,1:T(8,128)S(1)}) fusion(bf16[2048,1,128]{2,0,1:T(8,128)(2,1)} %get-tuple-element.383, bf16[608,1,8,128]{3,0,2,1:T(8,128)(2,1)S(1)} %get-tuple-element.382, s32[]{:T(128)} %get-tuple-element.363, s32[608]{0:T(1024)S(1)} %get-tuple-element.388, pred[2048]{0:T(1024)(128)(4,1)} %get-tuple-element.387, ...), kind=kOutput, calls=%fused_computation.69.clone.1 | convolution fusion | flops 329973152 | bytes 5680100 | tf_op jit(solution)/shard_map/while/body/eval_jaxpr/rhd,khd->rhk/dot_general | solution.py:90
  162.8 5.0 %fusion.77 = f32[2048,1,128]{0,2,1:T(8,128)} fusion(f32[2048,1,128]{0,2,1:T(8,128)} %get-tuple-element.366, pred[]{:T(512)S(6)} %compare.3, bf16[608,1,8,128]{3,0,2,1:T(8,128)(2,1)S(1)} %get-tuple-element.384, s32[]{:T(128)} %get-tuple-element.363, f32[608,1,2048]{2,0,1:T(8,128)} %copy-done, f32[608]{0:T(1024)S(1)} %fusion.72, ...), kind=kOutput, calls=%fused_computation.25.clone.1 | convolution fusion | flops 323026944 | bytes 7241733 | tf_op jit(solution)/shard_map/while/body/eval_jaxpr/rhk,rhd->khd/dot_general | solution.py:112
  173.0 3.6 %fusion.71 = (f32[608]{0:T(1024)S(1)}, f32[608,1,2048]{2,0,1:T(8,128)S(1)}) fusion(bf16[2048,1,128]{2,0,1:T(8,128)(2,1)} %get-tuple-element.383, bf16[608,1,8,128]{3,0,2,1:T(8,128)(2,1)S(1)} %get-tuple-element.382, s32[]{:T(128)} %get-tuple-element.363, s32[608]{0:T(1024)S(1)} %get-tuple-element.388, pred[2048]{0:T(1024)(128)(4,1)} %get-tuple-element.387, ...), kind=kOutput, calls=%fused_computation.69.clone.1 | convolution fusion | flops 329973152 | bytes 5680100 | tf_op jit(solution)/shard_map/while/body/eval_jaxpr/rhd,khd->rhk/dot_general | solution.py:90
  179.7 5.0 %fusion.77 = f32[2048,1,128]{0,2,1:T(8,128)} fusion(f32[2048,1,128]{0,2,1:T(8,128)} %get-tuple-element.366, pred[]{:T(512)S(6)} %compare.3, bf16[608,1,8,128]{3,0,2,1:T(8,128)(2,1)S(1)} %get-tuple-element.384, s32[]{:T(128)} %get-tuple-element.363, f32[608,1,2048]{2,0,1:T(8,128)} %copy-done, f32[608]{0:T(1024)S(1)} %fusion.72, ...), kind=kOutput, calls=%fused_computation.25.clone.1 | convolution fusion | flops 323026944 | bytes 7241733 | tf_op jit(solution)/shard_map/while/body/eval_jaxpr/rhk,rhd->khd/dot_general | solution.py:112
  189.8 3.6 %fusion.71 = (f32[608]{0:T(1024)S(1)}, f32[608,1,2048]{2,0,1:T(8,128)S(1)}) fusion(bf16[2048,1,128]{2,0,1:T(8,128)(2,1)} %get-tuple-element.383, bf16[608,1,8,128]{3,0,2,1:T(8,128)(2,1)S(1)} %get-tuple-element.382, s32[]{:T(128)} %get-tuple-element.363, s32[608]{0:T(1024)S(1)} %get-tuple-element.388, pred[2048]{0:T(1024)(128)(4,1)} %get-tuple-element.387, ...), kind=kOutput, calls=%fused_computation.69.clone.1 | convolution fusion | flops 329973152 | bytes 5680100 | tf_op jit(solution)/shard_map/while/body/eval_jaxpr/rhd,khd->rhk/dot_general | solution.py:90
  196.5 5.0 %fusion.77 = f32[2048,1,128]{0,2,1:T(8,128)} fusion(f32[2048,1,128]{0,2,1:T(8,128)} %get-tuple-element.366, pred[]{:T(512)S(6)} %compare.3, bf16[608,1,8,128]{3,0,2,1:T(8,128)(2,1)S(1)} %get-tuple-element.384, s32[]{:T(128)} %get-tuple-element.363, f32[608,1,2048]{2,0,1:T(8,128)} %copy-done, f32[608]{0:T(1024)S(1)} %fusion.72, ...), kind=kOutput, calls=%fused_computation.25.clone.1 | convolution fusion | flops 323026944 | bytes 7241733 | tf_op jit(solution)/shard_map/while/body/eval_jaxpr/rhk,rhd->khd/dot_general | solution.py:112
  206.7 3.6 %fusion.71 = (f32[608]{0:T(1024)S(1)}, f32[608,1,2048]{2,0,1:T(8,128)S(1)}) fusion(bf16[2048,1,128]{2,0,1:T(8,128)(2,1)} %get-tuple-element.383, bf16[608,1,8,128]{3,0,2,1:T(8,128)(2,1)S(1)} %get-tuple-element.382, s32[]{:T(128)} %get-tuple-element.363, s32[608]{0:T(1024)S(1)} %get-tuple-element.388, pred[2048]{0:T(1024)(128)(4,1)} %get-tuple-element.387, ...), kind=kOutput, calls=%fused_computation.69.clone.1 | convolution fusion | flops 329973152 | bytes 5680100 | tf_op jit(solution)/shard_map/while/body/eval_jaxpr/rhd,khd->rhk/dot_general | solution.py:90
  213.4 5.0 %fusion.77 = f32[2048,1,128]{0,2,1:T(8,128)} fusion(f32[2048,1,128]{0,2,1:T(8,128)} %get-tuple-element.366, pred[]{:T(512)S(6)} %compare.3, bf16[608,1,8,128]{3,0,2,1:T(8,128)(2,1)S(1)} %get-tuple-element.384, s32[]{:T(128)} %get-tuple-element.363, f32[608,1,2048]{2,0,1:T(8,128)} %copy-done, f32[608]{0:T(1024)S(1)} %fusion.72, ...), kind=kOutput, calls=%fused_computation.25.clone.1 | convolution fusion | flops 323026944 | bytes 7241733 | tf_op jit(solution)/shard_map/while/body/eval_jaxpr/rhk,rhd->khd/dot_general | solution.py:112
  223.5 3.6 %fusion.71 = (f32[608]{0:T(1024)S(1)}, f32[608,1,2048]{2,0,1:T(8,128)S(1)}) fusion(bf16[2048,1,128]{2,0,1:T(8,128)(2,1)} %get-tuple-element.383, bf16[608,1,8,128]{3,0,2,1:T(8,128)(2,1)S(1)} %get-tuple-element.382, s32[]{:T(128)} %get-tuple-element.363, s32[608]{0:T(1024)S(1)} %get-tuple-element.388, pred[2048]{0:T(1024)(128)(4,1)} %get-tuple-element.387, ...), kind=kOutput, calls=%fused_computation.69.clone.1 | convolution fusion | flops 329973152 | bytes 5680100 | tf_op jit(solution)/shard_map/while/body/eval_jaxpr/rhd,khd->rhk/dot_general | solution.py:90
  230.2 5.0 %fusion.77 = f32[2048,1,128]{0,2,1:T(8,128)} fusion(f32[2048,1,128]{0,2,1:T(8,128)} %get-tuple-element.366, pred[]{:T(512)S(6)} %compare.3, bf16[608,1,8,128]{3,0,2,1:T(8,128)(2,1)S(1)} %get-tuple-element.384, s32[]{:T(128)} %get-tuple-element.363, f32[608,1,2048]{2,0,1:T(8,128)} %copy-done, f32[608]{0:T(1024)S(1)} %fusion.72, ...), kind=kOutput, calls=%fused_computation.25.clone.1 | convolution fusion | flops 323026944 | bytes 7241733 | tf_op jit(solution)/shard_map/while/body/eval_jaxpr/rhk,rhd->khd/dot_general | solution.py:112
  240.4 3.7 %fusion.71 = (f32[608]{0:T(1024)S(1)}, f32[608,1,2048]{2,0,1:T(8,128)S(1)}) fusion(bf16[2048,1,128]{2,0,1:T(8,128)(2,1)} %get-tuple-element.383, bf16[608,1,8,128]{3,0,2,1:T(8,128)(2,1)S(1)} %get-tuple-element.382, s32[]{:T(128)} %get-tuple-element.363, s32[608]{0:T(1024)S(1)} %get-tuple-element.388, pred[2048]{0:T(1024)(128)(4,1)} %get-tuple-element.387, ...), kind=kOutput, calls=%fused_computation.69.clone.1 | convolution fusion | flops 329973152 | bytes 5680100 | tf_op jit(solution)/shard_map/while/body/eval_jaxpr/rhd,khd->rhk/dot_general | solution.py:90
  247.1 5.0 %fusion.77 = f32[2048,1,128]{0,2,1:T(8,128)} fusion(f32[2048,1,128]{0,2,1:T(8,128)} %get-tuple-element.366, pred[]{:T(512)S(6)} %compare.3, bf16[608,1,8,128]{3,0,2,1:T(8,128)(2,1)S(1)} %get-tuple-element.384, s32[]{:T(128)} %get-tuple-element.363, f32[608,1,2048]{2,0,1:T(8,128)} %copy-done, f32[608]{0:T(1024)S(1)} %fusion.72, ...), kind=kOutput, calls=%fused_computation.25.clone.1 | convolution fusion | flops 323026944 | bytes 7241733 | tf_op jit(solution)/shard_map/while/body/eval_jaxpr/rhk,rhd->khd/dot_general | solution.py:112
  264.8 55.4 %reduce-scatter.2.cloned.1.call-done = f32[96,256]{1,0:T(8,128)} async-done(((f32[1536,256]{1,0:T(8,128)}), f32[96,256]{1,0:T(8,128)}) %reduce-scatter.2.cloned.1.call-update) | async-done | bytes 98320 | tf_op jit(solution)/shard_map/reduce_scatter | solution.py:132
  (187 shorter events, 80.7 us)
Async XLA Ops:
  7.2 313.0 %reduce-scatter.2.cloned.1.call-start = ((), (), s32[]{:S(2)}) async-start(), calls=%async_computation.1 | async-start | bytes 1671168 | tf_op jit(solution)/shard_map/reduce_scatter | solution.py:132
  75.6 22.0 %copy-start.11 = (bf16[96,128]{1,0:T(8,128)(2,1)S(1)}, bf16[96,128]{1,0:T(8,128)(2,1)}, u32[]{:S(2)}) copy-start(bf16[96,128]{1,0:T(8,128)(2,1)} %param.19) | copy-start | bytes 73732
  75.6 45.5 %copy-start.8 = (bf16[512,128]{1,0:T(8,128)(2,1)S(1)}, bf16[512,128]{1,0:T(8,128)(2,1)}, u32[]{:S(2)}) copy-start(bf16[512,128]{1,0:T(8,128)(2,1)} %param.14) | copy-start | bytes 393220
  75.9 46.0 %copy-start.9 = (bf16[512,128]{1,0:T(8,128)(2,1)S(1)}, bf16[512,128]{1,0:T(8,128)(2,1)}, u32[]{:S(2)}) copy-start(bf16[512,128]{1,0:T(8,128)(2,1)} %param.15) | copy-start | bytes 393220
  129.4 4.7 %copy-start.1 = (f32[608,1,2048]{2,0,1:T(8,128)S(1)}, f32[608,1,2048]{2,0,1:T(8,128)}, u32[]{:S(2)}) copy-start(f32[608,1,2048]{2,0,1:T(8,128)} %copy-done) | copy-start | bytes 14942212 | tf_op jit(solution)/shard_map/while
  129.4 4.7 %copy-start.6 = (bf16[2048,1,128]{2,0,1:T(8,128)(2,1)S(1)}, bf16[2048,1,128]{2,0,1:T(8,128)(2,1)}, u32[]{:S(2)}) copy-start(bf16[2048,1,128]{2,0,1:T(8,128)(2,1)} %get-tuple-element.385) | copy-start | bytes 1572868 | tf_op jit(solution)/shard_map/while
  139.3 3.7 %copy-start.12 = (s32[608]{0:T(1024)}, s32[608]{0:T(1024)S(1)}, u32[]{:S(2)}) copy-start(s32[608]{0:T(1024)S(1)} %get-tuple-element.388) | copy-start | bytes 7300 | tf_op jit(solution)/shard_map/while
  146.0 5.0 %copy-start.1 = (f32[608,1,2048]{2,0,1:T(8,128)S(1)}, f32[608,1,2048]{2,0,1:T(8,128)}, u32[]{:S(2)}) copy-start(f32[608,1,2048]{2,0,1:T(8,128)} %copy-done) | copy-start | bytes 14942212 | tf_op jit(solution)/shard_map/while
  146.0 5.0 %copy-start.6 = (bf16[2048,1,128]{2,0,1:T(8,128)(2,1)S(1)}, bf16[2048,1,128]{2,0,1:T(8,128)(2,1)}, u32[]{:S(2)}) copy-start(bf16[2048,1,128]{2,0,1:T(8,128)(2,1)} %get-tuple-element.385) | copy-start | bytes 1572868 | tf_op jit(solution)/shard_map/while
  156.1 3.7 %copy-start.12 = (s32[608]{0:T(1024)}, s32[608]{0:T(1024)S(1)}, u32[]{:S(2)}) copy-start(s32[608]{0:T(1024)S(1)} %get-tuple-element.388) | copy-start | bytes 7300 | tf_op jit(solution)/shard_map/while
  162.8 5.0 %copy-start.1 = (f32[608,1,2048]{2,0,1:T(8,128)S(1)}, f32[608,1,2048]{2,0,1:T(8,128)}, u32[]{:S(2)}) copy-start(f32[608,1,2048]{2,0,1:T(8,128)} %copy-done) | copy-start | bytes 14942212 | tf_op jit(solution)/shard_map/while
  162.8 5.0 %copy-start.6 = (bf16[2048,1,128]{2,0,1:T(8,128)(2,1)S(1)}, bf16[2048,1,128]{2,0,1:T(8,128)(2,1)}, u32[]{:S(2)}) copy-start(bf16[2048,1,128]{2,0,1:T(8,128)(2,1)} %get-tuple-element.385) | copy-start | bytes 1572868 | tf_op jit(solution)/shard_map/while
  179.6 5.0 %copy-start.1 = (f32[608,1,2048]{2,0,1:T(8,128)S(1)}, f32[608,1,2048]{2,0,1:T(8,128)}, u32[]{:S(2)}) copy-start(f32[608,1,2048]{2,0,1:T(8,128)} %copy-done) | copy-start | bytes 14942212 | tf_op jit(solution)/shard_map/while
  179.6 5.0 %copy-start.6 = (bf16[2048,1,128]{2,0,1:T(8,128)(2,1)S(1)}, bf16[2048,1,128]{2,0,1:T(8,128)(2,1)}, u32[]{:S(2)}) copy-start(bf16[2048,1,128]{2,0,1:T(8,128)(2,1)} %get-tuple-element.385) | copy-start | bytes 1572868 | tf_op jit(solution)/shard_map/while
  196.5 5.0 %copy-start.1 = (f32[608,1,2048]{2,0,1:T(8,128)S(1)}, f32[608,1,2048]{2,0,1:T(8,128)}, u32[]{:S(2)}) copy-start(f32[608,1,2048]{2,0,1:T(8,128)} %copy-done) | copy-start | bytes 14942212 | tf_op jit(solution)/shard_map/while
  196.5 5.0 %copy-start.6 = (bf16[2048,1,128]{2,0,1:T(8,128)(2,1)S(1)}, bf16[2048,1,128]{2,0,1:T(8,128)(2,1)}, u32[]{:S(2)}) copy-start(bf16[2048,1,128]{2,0,1:T(8,128)(2,1)} %get-tuple-element.385) | copy-start | bytes 1572868 | tf_op jit(solution)/shard_map/while
  206.6 3.7 %copy-start.12 = (s32[608]{0:T(1024)}, s32[608]{0:T(1024)S(1)}, u32[]{:S(2)}) copy-start(s32[608]{0:T(1024)S(1)} %get-tuple-element.388) | copy-start | bytes 7300 | tf_op jit(solution)/shard_map/while
  213.3 5.0 %copy-start.1 = (f32[608,1,2048]{2,0,1:T(8,128)S(1)}, f32[608,1,2048]{2,0,1:T(8,128)}, u32[]{:S(2)}) copy-start(f32[608,1,2048]{2,0,1:T(8,128)} %copy-done) | copy-start | bytes 14942212 | tf_op jit(solution)/shard_map/while
  213.3 5.0 %copy-start.6 = (bf16[2048,1,128]{2,0,1:T(8,128)(2,1)S(1)}, bf16[2048,1,128]{2,0,1:T(8,128)(2,1)}, u32[]{:S(2)}) copy-start(bf16[2048,1,128]{2,0,1:T(8,128)(2,1)} %get-tuple-element.385) | copy-start | bytes 1572868 | tf_op jit(solution)/shard_map/while
  230.2 5.0 %copy-start.1 = (f32[608,1,2048]{2,0,1:T(8,128)S(1)}, f32[608,1,2048]{2,0,1:T(8,128)}, u32[]{:S(2)}) copy-start(f32[608,1,2048]{2,0,1:T(8,128)} %copy-done) | copy-start | bytes 14942212 | tf_op jit(solution)/shard_map/while
  230.2 5.0 %copy-start.6 = (bf16[2048,1,128]{2,0,1:T(8,128)(2,1)S(1)}, bf16[2048,1,128]{2,0,1:T(8,128)(2,1)}, u32[]{:S(2)}) copy-start(bf16[2048,1,128]{2,0,1:T(8,128)(2,1)} %get-tuple-element.385) | copy-start | bytes 1572868 | tf_op jit(solution)/shard_map/while
  240.4 3.7 %copy-start.12 = (s32[608]{0:T(1024)}, s32[608]{0:T(1024)S(1)}, u32[]{:S(2)}) copy-start(s32[608]{0:T(1024)S(1)} %get-tuple-element.388) | copy-start | bytes 7300 | tf_op jit(solution)/shard_map/while
  247.1 5.0 %copy-start.1 = (f32[608,1,2048]{2,0,1:T(8,128)S(1)}, f32[608,1,2048]{2,0,1:T(8,128)}, u32[]{:S(2)}) copy-start(f32[608,1,2048]{2,0,1:T(8,128)} %copy-done) | copy-start | bytes 14942212 | tf_op jit(solution)/shard_map/while
  247.1 5.0 %copy-start.6 = (bf16[2048,1,128]{2,0,1:T(8,128)(2,1)S(1)}, bf16[2048,1,128]{2,0,1:T(8,128)(2,1)}, u32[]{:S(2)}) copy-start(bf16[2048,1,128]{2,0,1:T(8,128)(2,1)} %get-tuple-element.385) | copy-start | bytes 1572868 | tf_op jit(solution)/shard_map/while
  (33 other events, 56.6 us)
Sparse Core Ops, SparseCore 0:
  260.2 59.9 reduce-scatter.1
where the time goes:
time: 330 us; the launch traced here: 329 us
  blocking collectives  100 us (30%)
  matrix products  97.5 us (30%)
  waiting for transfers between devices  55.4 us (17%)
  other arithmetic  29.8 us (9%)
  local copies, waits for them, and re-layouts  26.5 us (8%)
  between operations  18.2 us (6%)
    reduce_scatter x1, waiting for transfers between devices, per_device(): lax.psum_scatter(key_grads[:prompt_len], 'group', scatter_dimension=0, ti...  55.4 us
    dot_general x8, matrix products, head_terms(): jnp.einsum('rhk,rhd->khd', weights_b, cot_head, preferred_element_type=jn...  39.7 us
    psum x1, blocking collectives, per_device(): rewards = lax.psum(table, 'group')  37 us
    dot_general x8, matrix products, head_terms(): jnp.einsum('rhd,khd->rhk', query_head, key_rows, preferred_element_type=j...  29.1 us
    all_gather x1, blocking collectives, per_device(): lax.all_gather(prompt_value_array, 'group', axis=0, tiled=True)  23.5 us
    all_gather x1, blocking collectives, per_device(): lax.all_gather(prompt_key_array, 'group', axis=0, tiled=True)  21.3 us
    psum x1, blocking collectives, per_device(): own_count = lax.psum(local_count, 'tensor')  18.6 us
    while x96, local copies, waits for them, and re-layouts  17.7 us
  transfers between devices with their start and end apart: 1, of which 1 were waited for; matrix products, arithmetic and copies ran while one was open for 1% of the time, Pallas kernels for 0%

commit v1 on v0

v1 whole, which is shorter than its diff:
```python
import functools
import jax
import jax.numpy as jnp
from jax import lax
from jax.experimental import pallas as pl
from jax.experimental.pallas import tpu as pltpu
from jax.sharding import PartitionSpec as P

MESH = pl.DeviceIdType.MESH
NG, NT, TESTS, MAXB, BLK = 16, 8, 32, 4, 128
F32, BF = jnp.float32, jnp.bfloat16
HEADS, D, CR, PR, PK = 8, 128, 512, 96, 1536
NB = CR // 128
NK = PK + CR
SCALE = D ** -0.5
C2 = SCALE * 1.4426950408889634

def dot(a, b, ca=1, cb=0):
    return lax.dot_general(a, b, (((ca,), (cb,)), ((), ())), preferred_element_type=F32)

def split(x):
    xs = x.astype(F32) * C2
    hi = xs.astype(BF)
    lo = (xs - hi.astype(F32)).astype(BF)
    return hi, lo

def compute_kernel(len_ref, slot_ref, rew, qc, dc, qp, dp, kv, kc, vc,
           dqc, dkc, dvc, dqp, part,
           kk, kkt, vt, W, DS, QT, OT, S0, S1, S2, S3, S4, T0, T1, T2, T3, T4, cot):
    S = [S0, S1, S2, S3, S4]
    T = [T0, T1, T2, T3, T4]
    g = lax.axis_index("group")
    blocks = jnp.int32(0)
    for c in range(NG):
        blocks = blocks + jnp.where(slot_ref[c] == g, len_ref[c], 0)
    live = blocks * BLK
    center = jnp.sum(rew[...], axis=0, keepdims=True) / NG
    adv = rew[pl.ds(g, 1), :] - center
    fac = adv * MAXB / jnp.broadcast_to(blocks.astype(F32), (1, D))
    kk[:PK] = kv[:, :D]
    kk[PK:] = kc[...]
    kt = jnp.transpose(kk[...])
    kkt[:D] = kt
    kkt[D:] = kt
    vt[:, :PK] = jnp.transpose(kv[:, D:])
    vt[:, PK:] = jnp.transpose(vc[...])
    row = lax.broadcasted_iota(jnp.int32, (CR, 1), 0)
    f = jnp.where(row < live, fac, 0.0)
    @pl.loop(0, HEADS)
    def _(h):
        c = pl.ds(pl.multiple_of(h * D, D), D)
        ct = (dc[:, c].astype(F32) * f).astype(BF)
        cot[:, c] = ct
        ctt = jnp.transpose(ct)
        qt = jnp.transpose(qc[:, c])
        for i in range(NB):
            cc = pl.ds(pl.multiple_of(i * 1024 + h * D, D), D)
            OT[:, cc] = ctt[:, i * 128:(i + 1) * 128]
            QT[:, cc] = qt[:, i * 128:(i + 1) * 128]
    OT[:, 4096:] = jnp.transpose(jnp.concatenate([dp[:, h * D:(h + 1) * D] for h in range(HEADS)], axis=0))
    QT[:, 4096:] = jnp.transpose(jnp.concatenate([qp[:, h * D:(h + 1) * D] for h in range(HEADS)], axis=0))
    for i in (0, 2):
        W[i * 1024:(i + 1) * 1024, PK + (i + 1) * 128:PK + (i + 2) * 128] = jnp.zeros((1024, 128), BF)
        DS[i * 1024:(i + 1) * 1024, PK + (i + 1) * 128:PK + (i + 2) * 128] = jnp.zeros((1024, 128), BF)

    nks = [PK + 128 * (i + 1) for i in range(NB)] + [PK]

    def mm1(t, h):
        c = pl.ds(pl.multiple_of(h * D, D), D)
        if t < NB:
            q = qc[t * 128:(t + 1) * 128, c]
            o = cot[t * 128:(t + 1) * 128, c]
        else:
            q = qp[:, c]
            o = dp[:, c]
        hi, lo = split(q)
        S[t][...] = dot(jnp.concatenate([hi, lo], axis=1), kkt[:, :nks[t]])
        T[t][...] = dot(o, vt[:, :nks[t]])

    def soft(t, h):
        s = S[t][...]
        n = nks[t]
        if t < NB:
            r = lax.broadcasted_iota(jnp.int32, (128, 128), 0)
            k = lax.broadcasted_iota(jnp.int32, (128, 128), 1)
            s = jnp.concatenate([s[:, :n - 128], jnp.where(k <= r, s[:, n - 128:], -1e30)], axis=1)
        else:
            r = lax.broadcasted_iota(jnp.int32, (PR, n), 0) + g * PR
            k = lax.broadcasted_iota(jnp.int32, (PR, n), 1)
            s = jnp.where(k <= r, s, -1e30)
        m = jnp.max(s, axis=1, keepdims=True)
        e = jnp.exp2(s - m)
        tot = jnp.sum(e, axis=1, keepdims=True)
        w = e * (1.0 / tot)
        d = T[t][...]
        drift = jnp.sum(w * d, axis=1, keepdims=True)
        ds = (w * (d - drift)).astype(BF)
        if t < NB:
            rr = pl.ds(pl.multiple_of(t * 1024 + h * 128, 128), 128)
        else:
            rr = pl.ds(pl.multiple_of(4096 + h * PR, 32), PR)
        W[rr, :n] = w.astype(BF)
        DS[rr, :n] = ds
        return ds

    def mm2(t, h):
        c = pl.ds(pl.multiple_of(h * D, D), D)
        n = nks[t]
        if t < NB:
            rr = pl.ds(pl.multiple_of(t * 1024 + h * 128, 128), 128)
            dqc[t * 128:(t + 1) * 128, c] = (dot(DS[rr, :n], kk[:n]) * SCALE).astype(BF)
        else:
            rr = pl.ds(pl.multiple_of(4096 + h * PR, 32), PR)
            dqp[:, c] = (dot(DS[rr, :n], kk[:n]) * SCALE).astype(BF)

    mm1(0, 0)
    @pl.loop(0, HEADS)
    def _(h):
        for t in range(5):
            if t < 4:
                mm1(t + 1, h)
            else:
                mm1(0, lax.rem(h + 1, HEADS))
            soft(t, h)
            mm2(t, h)
    for b in range(NK // 256):
        lo, hi = b * 256, (b + 1) * 256
        if lo < PK:
            r0, r1 = 0, 4096 + HEADS * PR
        else:
            r0, r1 = ((lo - PK) // 128) * 1024, 4096
        gv = jnp.transpose(dot(OT[:, r0:r1], W[r0:r1, lo:hi])).astype(BF)
        gk = jnp.transpose(dot(QT[:, r0:r1], DS[r0:r1, lo:hi]) * SCALE).astype(BF)
        if lo < PK:
            part[lo:hi, :D] = gk
            part[lo:hi, D:] = gv
        else:
            dkc[lo - PK:hi - PK] = gk
            dvc[lo - PK:hi - PK] = gv

def compute(lengths, slot_of, rew, qc, dc, qp, dp, kv, kc, vc):
    v = pl.BlockSpec(memory_space=pltpu.VMEM)
    sm = pl.BlockSpec(memory_space=pltpu.SMEM)
    R = 4096 + HEADS * PR
    nks = [PK + 128 * (i + 1) for i in range(NB)] + [PK]
    rows = [128] * 4 + [PR]
    return pl.pallas_call(
        compute_kernel,
        out_shape=(jax.ShapeDtypeStruct((CR, 1024), BF), jax.ShapeDtypeStruct((CR, D), BF), jax.ShapeDtypeStruct((CR, D), BF),
                   jax.ShapeDtypeStruct((PR, 1024), BF), jax.ShapeDtypeStruct((PK, 2 * D), BF)),
        in_specs=[sm, sm] + [v] * 8, out_specs=[v] * 5,
        scratch_shapes=[pltpu.VMEM((NK, D), BF), pltpu.VMEM((2 * D, NK), BF), pltpu.VMEM((D, NK), BF),
                        pltpu.VMEM((R, NK), BF), pltpu.VMEM((R, NK), BF), pltpu.VMEM((D, R), BF), pltpu.VMEM((D, R), BF)]
                       + [pltpu.VMEM((r, n), F32) for r, n in zip(rows, nks)] * 2 + [pltpu.VMEM((CR, 1024), BF)],
        compiler_params=pltpu.CompilerParams(vmem_limit_bytes=63 << 20),
        name="attention_backward",
    )(lengths, slot_of, rew, qc, dc, qp, dp, kv, kc, vc)


def peers(g, t):
    chip, core = g // 2, lax.rem(g, 2)
    same = [(2 * lax.rem(chip + j, 8) + core, t) for j in range(1, 8)]
    sib = (2 * chip + 1 - core, t)
    return chip, core, same, sib


def gather_kernel(pk, pv, passes, kv, rew, own, cnt, cnt_in, rew_in, ss, rs, cs, cr, ws, wr):
    g, t = lax.axis_index("group"), lax.axis_index("tensor")
    chip, core, same, sib = peers(g, t)
    group = [(lax.rem(g + j, NG), t) for j in range(1, NG)]
    tens = [(g, lax.rem(t + j, NT)) for j in range(1, NT)]
    barrier = pltpu.get_barrier_semaphore()
    for d in group + tens:
        pl.semaphore_signal(barrier, inc=1, device_id=d, device_id_type=MESH)
    own[:, :D] = pk[...]
    own[:, D:] = pv[...]
    cnt[...] = jnp.broadcast_to(jnp.sum(passes[...].astype(F32), axis=1, keepdims=True), (8, D))
    pl.semaphore_wait(barrier, len(group) + len(tens))
    mine = pl.ds(pl.multiple_of(g * PR, 32), PR)

    def rc(src, dst, s, r, d):
        return pltpu.make_async_remote_copy(src_ref=src, dst_ref=dst, send_sem=s, recv_sem=r, device_id=d, device_id_type=MESH)

    c1 = [rc(cnt, cnt_in.at[j], cs.at[j], cr.at[j], tens[j]) for j in range(NT - 1)]
    for c in c1:
        c.start()
    out = [rc(own, kv.at[mine], ss.at[j], rs.at[j], same[j - 1] if j else sib) for j in range(8)]
    for c in out:
        c.start()
    kv[mine, :] = own[...]
    for c in c1:
        c.wait_recv()
    total = cnt[...]
    for j in range(NT - 1):
        total = total + cnt_in[j]
    r8 = total / TESTS
    rew_in[pl.ds(g, 1)] = r8[None]
    c2 = [rc(rew_in.at[pl.ds(g, 1)], rew_in.at[pl.ds(g, 1)], ws.at[j], wr.at[j], group[j]) for j in range(NG - 1)]
    for c in c2:
        c.start()
    fwd = []
    for j in range(1, 8):
        out[j].wait_recv()
        src = 2 * lax.rem(chip - j + 8, 8) + core
        rows = pl.ds(pl.multiple_of(src * PR, 32), PR)
        f = rc(kv.at[rows], kv.at[rows], ss.at[7 + j], rs.at[7 + j], sib)
        f.start()
        fwd.append(f)
    for c in c2:
        c.wait_recv()
    for s in range(NG):
        rew[s:s + 1, :] = rew_in[s][:1]
    out[0].wait_recv()
    for f in fwd:
        f.wait_recv()
    for c in c1 + out + c2 + fwd:
        c.wait_send()


def gather(pk, pv, passes):
    v = pl.BlockSpec(memory_space=pltpu.VMEM)
    dma = pltpu.SemaphoreType.DMA
    return pl.pallas_call(
        gather_kernel,
        out_shape=(jax.ShapeDtypeStruct((PK, 2 * D), BF), jax.ShapeDtypeStruct((NG, D), F32)),
        in_specs=[v] * 3, out_specs=[v] * 2,
        scratch_shapes=[pltpu.VMEM((PR, 2 * D), BF), pltpu.VMEM((8, D), F32), pltpu.VMEM((NT - 1, 8, D), F32), pltpu.VMEM((NG, 8, D), F32),
                        dma((15,)), dma((15,)), dma((NT - 1,)), dma((NT - 1,)), dma((NG - 1,)), dma((NG - 1,))],
        compiler_params=pltpu.CompilerParams(collective_id=1, has_side_effects=True),
        name="gather_prompt",
    )(pk, pv, passes)


def scatter_kernel(part, dk, dv, inc, summed, got, s1, r1, s2, r2):
    g, t = lax.axis_index("group"), lax.axis_index("tensor")
    chip, core, same, sib = peers(g, t)
    barrier = pltpu.get_barrier_semaphore()
    for d in same + [sib]:
        pl.semaphore_signal(barrier, inc=1, device_id=d, device_id_type=MESH)
    pl.semaphore_wait(barrier, 8)

    def rows(c, k):
        return pl.ds(pl.multiple_of((2 * c + k) * PR, 32), PR)

    def rc(src, dst, s, r, d):
        return pltpu.make_async_remote_copy(src_ref=src, dst_ref=dst, send_sem=s, recv_sem=r, device_id=d, device_id_type=MESH)

    order = [1, 2, 3, 4, 5, 6, 7, 0]
    chips = [lax.rem(chip + j, 8) for j in order]
    first = [rc(part.at[rows(chips[i], 1 - core)], inc.at[i], s1.at[i], r1.at[i], sib) for i in range(8)]
    for c in first:
        c.start()
    second = []
    for i in range(8):
        first[i].wait_recv()
        x = inc[i].astype(F32) + part[rows(chips[i], core), :].astype(F32)
        if i < 7:
            summed[i] = x.astype(BF)
            c = rc(summed.at[i], got.at[i], s2.at[i], r2.at[i], same[i])
            c.start()
            second.append(c)
        else:
            total = x
    for i in range(7):
        second[i].wait_recv()
        total = total + got[i].astype(F32)
    dk[...] = total[:, :D].astype(BF)
    dv[...] = total[:, D:].astype(BF)
    for c in first + second:
        c.wait_send()


def scatter(part):
    v = pl.BlockSpec(memory_space=pltpu.VMEM)
    dma = pltpu.SemaphoreType.DMA
    return pl.pallas_call(
        scatter_kernel,
        out_shape=(jax.ShapeDtypeStruct((PR, D), BF), jax.ShapeDtypeStruct((PR, D), BF)),
        in_specs=[v], out_specs=[v] * 2,
        scratch_shapes=[pltpu.VMEM((8, PR, 2 * D), BF), pltpu.VMEM((7, PR, 2 * D), BF), pltpu.VMEM((7, PR, 2 * D), BF),
                        dma((8,)), dma((8,)), dma((7,)), dma((7,))],
        compiler_params=pltpu.CompilerParams(collective_id=2, has_side_effects=True),
        name="scatter_prompt",
    )(part)


def per_device(qc, kc, vc, dc, qp, pk, pv, dp, lengths, slot_of, passes):
    kv, rew = gather(pk, pv, passes)
    dqc, dkc, dvc, dqp, part = compute(lengths, slot_of, rew, qc, dc, qp, dp, kv, kc, vc)
    dk, dv = scatter(part)
    return dqc, dkc, dvc, dqp, dk, dv


def solution(mesh):
    gt = P("group", "tensor")
    return jax.shard_map(per_device, mesh=mesh, in_specs=(gt,) * 8 + (P(), P(), gt), out_specs=(gt,) * 6, check_vma=False)
```

time: 330 us -> 73.4 us (0.22)
  blocking collectives: 100 us -> 0 us
  matrix products: 97.5 us -> 0 us
  Pallas kernels: 0 us -> 70.5 us
  waiting for transfers between devices: 55.4 us -> 0 us
  other arithmetic: 29.8 us -> 0 us
  local copies, waits for them, and re-layouts: 26.5 us -> 1.96 us
  between operations: 18.2 us -> 0.66 us
    dot_general x40 -> x0, matrix products: 97.5 us -> none  [the longest x8 39.7 us: head_terms(): jnp.einsum('rhk,rhd->khd', weights_b, cot_head, preferred_element_type=jn...]
    pallas_call x0 -> x3, Pallas kernels: none -> 70.5 us  [the longest x1 35.2 us: compute(): pl.pallas_call(compute_kernel, out_shape=(jax.ShapeDtypeStruct((CR, 1024)...]
    psum x2 -> x0, blocking collectives: 55.5 us -> none  [the longest x1 37 us: per_device(): rewards = lax.psum(table, 'group')]
    reduce_scatter x1 -> x0, waiting for transfers between devices: 55.4 us -> none  [per_device(): lax.psum_scatter(key_grads[:prompt_len], 'group', scatter_dimension=0, ti...]
    all_gather x2 -> x0, blocking collectives: 44.8 us -> none  [the longest x1 23.5 us: per_device(): lax.all_gather(prompt_value_array, 'group', axis=0, tiled=True)]
    while x98 -> x0, local copies, waits for them, and re-layouts: 18.4 us -> none
    another operation x9 -> x0, other arithmetic: 12.8 us -> none
    reduce_sum x12 -> x0, other arithmetic: 10.3 us -> none  [the longest x8 6.48 us: head_terms(): row_total = jnp.sum(exps, axis=2, keepdims=True)]
  transfers between devices with their start and end apart: 1 -> 0, of which waited for: 1 -> 0; matrix products, arithmetic and copies ran while one was open for 1% -> 0% of each run, Pallas kernels for 0% -> 0%
where the time goes in v1:
time: 73.4 us; the launch traced here: 73.1 us
  Pallas kernels  70.5 us (96%)
  local copies, waits for them, and re-layouts  1.96 us (3%)
    pallas_call x1, Pallas kernels, compute(): pl.pallas_call(compute_kernel, out_shape=(jax.ShapeDtypeStruct((CR, 1024)...  35.2 us
    pallas_call x1, Pallas kernels, gather(): pl.pallas_call(gather_kernel, out_shape=(jax.ShapeDtypeStruct((PK, 2 * D)...  21.2 us
    pallas_call x1, Pallas kernels, scatter(): pl.pallas_call(scatter_kernel, out_shape=(jax.ShapeDtypeStruct((PR, D), B...  14 us
    unnamed x4, local copies, waits for them, and re-layouts  1.96 us

profile of v1, /device:TPU:1, one launch (start us, length us, event | category | flops | bytes accessed | tf_op | source)
XLA Modules:
  0.0 73.1 jit_solution(15025154533056353625)
XLA Ops:
  0.6 21.2 %gather_prompt.1 = (bf16[1536,256]{1,0:T(8,128)(2,1)}, f32[16,128]{1,0:T(8,128)}) custom-call(bf16[96,128]{1,0:T(8,128)(2,1)} %pk.1, bf16[96,128]{1,0:T(8,128)(2,1)} %pv.1, s32[1,4]{1,0:T(1,128)} %passes.1), custom_call_target="tpu_custom_call" | custom-call | tf_op jit(solution)/shard_map/gather_prompt/pallas_call | solution.py:223
  21.9 35.2 %attention_backward.1 = (bf16[512,1024]{1,0:T(8,128)(2,1)}, bf16[512,128]{1,0:T(8,128)(2,1)}, bf16[512,128]{1,0:T(8,128)(2,1)}, bf16[96,1024]{1,0:T(8,128)(2,1)}, bf16[1536,256]{1,0:T(8,128)(2,1)}) custom-call(s32[16]{0:T(128)} %len_ref.1, s32[16]{0:T(128)} %slot_ref.1, f32[16,128]{1,0:T(8,128)} %get-tuple-element.15.rew, bf16[512,1024]{1,0:T(8,128)(2,1)} %qc.1, ...), custom_call_target="tpu_custom_call" | custom-call | tf_op jit(solution)/shard_map/attention_backward/pallas_call | solution.py:147
  57.1 14.0 %scatter_prompt.1 = (bf16[96,128]{1,0:T(8,128)(2,1)}, bf16[96,128]{1,0:T(8,128)(2,1)}) custom-call(bf16[1536,256]{1,0:T(8,128)(2,1)} %get-tuple-element.21.part), custom_call_target="tpu_custom_call" | custom-call | tf_op jit(solution)/shard_map/scatter_prompt/pallas_call | solution.py:276
  71.2 0.0 copy-start
  71.2 1.4 %copy.19 = bf16[96,128]{1,0:T(8,128)(2,1)} copy(bf16[96,128]{1,0:T(8,128)(2,1)} %get-tuple-element.34) | data formatting | bytes 49152
  72.5 0.0 copy-done
  72.5 0.6 copy.20
Async XLA Ops:
  71.2 1.4 %copy-start = (bf16[96,128]{1,0:T(8,128)(2,1)S(1)}, bf16[96,128]{1,0:T(8,128)(2,1)}, u32[]{:S(2)}) copy-start(bf16[96,128]{1,0:T(8,128)(2,1)} %get-tuple-element.35) | copy-start | bytes 73732

commit v2 on v0

v2 whole, which is shorter than its diff:
```python
import jax
import jax.numpy as jnp
from jax import lax
from jax.experimental import pallas as pl
from jax.experimental.pallas import tpu as pltpu
from jax.sharding import PartitionSpec as P

MESH = pl.DeviceIdType.MESH
NG, NT, TESTS, MAXB, BLK = 16, 8, 32, 4, 128
F32, BF = jnp.float32, jnp.bfloat16
HEADS, D, CR, PR, PK = 8, 128, 512, 96, 1536
NB = CR // 128
NK = PK + CR
RC = HEADS * CR
RA = RC + HEADS * PR
SCALE = D ** -0.5
C2 = SCALE * 1.4426950408889634
NKS = [PK + 128 * (i + 1) for i in range(NB)] + [PK]
ROWS = [128] * NB + [PR]
CHIPS = NG // 2


def dot(a, b):
    return lax.dot_general(a, b, (((1,), (0,)), ((), ())), preferred_element_type=F32)


def backward_kernel(qc_h, kc_h, vc_h, dc_h, qp_h, pk_h, pv_h, dp_h, len_h, slot_h, passes_h,
                    dqc_h, dkc_h, dvc_h, dqp_h, dk_h, dv_h,
                    qc, dc, qp, dp, lens, slots, passes, kv, kc, vc, kk, kkt, vt, W, DS, QT, OT, RF, QP, OP,
                    dqc, dqp, dkc, dvc, dk, dv, part, inc, summed, got, cnt, cnt_in, rew,
                    S0, S1, S2, S3, S4, T0, T1, T2, T3, T4,
                    ls, os, gs, gr, cs, cr, ws, wr, s1, r1, s2, r2):
    S, T = [S0, S1, S2, S3, S4], [T0, T1, T2, T3, T4]
    g, t_ax = lax.axis_index("group"), lax.axis_index("tensor")
    chip, core = g // 2, lax.rem(g, 2)
    same = [(2 * lax.rem(chip + j, CHIPS) + core, t_ax) for j in range(1, CHIPS)]
    sib = (2 * chip + 1 - core, t_ax)
    group = [(lax.rem(g + j, NG), t_ax) for j in range(1, NG)]
    tens = [(g, lax.rem(t_ax + j, NT)) for j in range(1, NT)]

    def rc(src, dst, s, r, d):
        return pltpu.make_async_remote_copy(src_ref=src, dst_ref=dst, send_sem=s, recv_sem=r, device_id=d, device_id_type=MESH)

    def shard(s):
        return pl.ds(pl.multiple_of(s * PR, 32), PR)

    barrier = pltpu.get_barrier_semaphore()
    for d in group + tens:
        pl.semaphore_signal(barrier, inc=1, device_id=d, device_id_type=MESH)
    mine = shard(g)
    loads = [pltpu.make_async_copy(a, b, ls.at[i]) for i, (a, b) in enumerate([
        (pk_h, kv.at[mine, pl.ds(0, D)]), (pv_h, kv.at[mine, pl.ds(D, D)]), (passes_h, passes), (kc_h, kc), (vc_h, vc),
        (len_h, lens), (slot_h, slots), (qc_h, qc), (dc_h, dc), (qp_h, qp), (dp_h, dp)])]
    for c in loads:
        c.start()
    for i in range(0, NB, 2):
        z = jnp.zeros((1024, 128), BF)
        W[i * 1024:(i + 1) * 1024, PK + (i + 1) * 128:PK + (i + 2) * 128] = z
        DS[i * 1024:(i + 1) * 1024, PK + (i + 1) * 128:PK + (i + 2) * 128] = z
    for c in loads:
        c.wait()
    cnt[...] = jnp.broadcast_to(jnp.sum(passes[...].astype(F32), axis=1, keepdims=True), (8, D))
    kk[PK:] = kc[...]
    kt = jnp.transpose(kc[...])
    kkt[:D, PK:] = kt
    kkt[D:, PK:] = kt
    vt[:, PK:] = jnp.transpose(vc[...])
    pl.semaphore_wait(barrier, len(group) + len(tens))

    c1 = [rc(cnt, cnt_in.at[j], cs.at[j], cr.at[j], tens[j]) for j in range(NT - 1)]
    out = [rc(kv.at[mine], kv.at[mine], gs.at[j], gr.at[j], same[j - 1] if j else sib) for j in range(CHIPS)]
    for c in c1 + out:
        c.start()
    for c in c1:
        c.wait_recv()
    total = cnt[...]
    for j in range(NT - 1):
        total = total + cnt_in[j]
    rew[pl.ds(g, 1)] = (total / TESTS)[None]
    c2 = [rc(rew.at[pl.ds(g, 1)], rew.at[pl.ds(g, 1)], ws.at[j], wr.at[j], group[j]) for j in range(NG - 1)]
    for c in c2:
        c.start()
    fwd = []
    for j in range(1, CHIPS):
        out[j].wait_recv()
        rows = shard(2 * lax.rem(chip - j + CHIPS, CHIPS) + core)
        f = rc(kv.at[rows], kv.at[rows], gs.at[CHIPS - 1 + j], gr.at[CHIPS - 1 + j], sib)
        f.start()
        fwd.append(f)
    out[0].wait_recv()
    for f in fwd:
        f.wait_recv()
    kp = kv[:, :D]
    kk[:PK] = kp
    kt = jnp.transpose(kp)
    kkt[:D, :PK] = kt
    kkt[D:, :PK] = kt
    vt[:, :PK] = jnp.transpose(kv[:, D:])

    def cols(h):
        return pl.ds(pl.multiple_of(h * D, D), D)

    def rows_of(t, h):
        if t < NB:
            return pl.multiple_of(t * 1024 + h * 128, 128)
        return pl.multiple_of(RC + h * PR, 32)

    def qo(t, h):
        c = cols(h)
        if t < NB:
            return qc[t * 128:(t + 1) * 128, c], dc[t * 128:(t + 1) * 128, c]
        return qp[:, c], dp[:, c]

    def products(t, h):
        q, o = qo(t, h)
        n = NKS[t]
        xs = q.astype(F32) * C2
        hi = xs.astype(BF)
        lo = (xs - hi.astype(F32)).astype(BF)
        s = dot(jnp.concatenate([hi, lo], axis=1), kkt[:, :n])
        if t < NB:
            r = lax.broadcasted_iota(jnp.int32, (128, 128), 0)
            k = lax.broadcasted_iota(jnp.int32, (128, 128), 1)
            s = jnp.concatenate([s[:, :n - 128], jnp.where(k <= r, s[:, n - 128:], -1e30)], axis=1)
        else:
            r = lax.broadcasted_iota(jnp.int32, s.shape, 0) + g * PR
            k = lax.broadcasted_iota(jnp.int32, s.shape, 1)
            s = jnp.where(k <= r, s, -1e30)
        S[t][...] = s
        T[t][...] = dot(o, vt[:, :n])

    products(0, 0)
    for c in c2:
        c.wait_recv()
    center = rew[0]
    for s in range(1, NG):
        center = center + rew[s]
    blocks = jnp.sum(jnp.where(slots[...] == g, lens[...], 0).astype(F32), axis=1, keepdims=True)
    adv = rew[pl.ds(g, 1)][0][:1] - (center / NG)[:1]
    fac = adv * MAXB / blocks
    live = blocks * BLK

    def softmax(t, h):
        n = NKS[t]
        rr = rows_of(t, h)
        s = S[t][...]
        m = jnp.max(s, axis=1, keepdims=True)
        e = jnp.exp2(s - m)
        tot = jnp.sum(e, axis=1, keepdims=True)
        d = T[t][...]
        r = 1.0 / tot
        drift = jnp.sum(e * d, axis=1, keepdims=True) * r
        out = pl.ds(rr, ROWS[t])
        W[out, :n] = e.astype(BF)
        DS[out, :n] = (e * (d - drift)).astype(BF)
        if t < NB:
            row = lax.broadcasted_iota(jnp.int32, (128, D), 0) + t * 128
            r = r * jnp.where(row.astype(F32) < live, fac, 0.0)
        else:
            r = jnp.broadcast_to(r, (PR, D))
        RF[out, :] = r * SCALE
        q, o = qo(t, h)
        qs = (q.astype(F32) * (r * SCALE)).astype(BF)
        os_ = (o.astype(F32) * r).astype(BF)
        if t < NB:
            c = pl.ds(rr, 128)
            QT[:, c] = jnp.transpose(qs)
            OT[:, c] = jnp.transpose(os_)
        else:
            c = pl.ds(rr - RC, PR)
            QP[c, :] = qs
            OP[c, :] = os_

    @pl.loop(0, HEADS)
    def _(h):
        for t in range(5):
            if t < 4:
                products(t + 1, h)
            else:
                products(0, lax.rem(h + 1, HEADS))
            softmax(t, h)
    QT[:, RC:] = jnp.transpose(QP[...])
    OT[:, RC:] = jnp.transpose(OP[...])

    def key_block(b):
        lo, hi = b * 256, (b + 1) * 256
        r0, r1_ = (0, RA) if lo < PK else (((lo - PK) // 128) * 1024, RC)
        gv = jnp.transpose(dot(OT[:, r0:r1_], W[r0:r1_, lo:hi])).astype(BF)
        gk = jnp.transpose(dot(QT[:, r0:r1_], DS[r0:r1_, lo:hi])).astype(BF)
        if lo < PK:
            part[lo:hi, :D] = gk
            part[lo:hi, D:] = gv
        else:
            dkc[lo - PK:hi - PK] = gk
            dvc[lo - PK:hi - PK] = gv

    first = [rc(part.at[shard(2 * c + 1 - core)], inc.at[c], s1.at[c], r1.at[c], sib) for c in range(CHIPS)]
    second = [rc(summed.at[c], got.at[chip], s2.at[c], r2.at[chip], (2 * c + core, t_ax)) for c in range(CHIPS)]

    def pass_on(c):
        first[c].wait_recv()
        x = inc[c].astype(F32) + part[shard(2 * c + core), :].astype(F32)
        summed[c] = x.astype(BF)
        pl.when(chip != c)(second[c].start)

    started = 0
    for b in range(PK // 256):
        key_block(b)
        ready = ((b + 1) * 256 // PR) // 2
        for c in range(started, ready):
            first[c].start()
        if b:
            for c in range(passed, started):
                pass_on(c)
        passed, started = started, ready
    for b in range(PK // 256, NK // 256):
        key_block(b)
    for c in range(passed, CHIPS):
        pass_on(c)

    stores = [pltpu.make_async_copy(a, b, os.at[i]) for i, (a, b) in enumerate([
        (dkc, dkc_h), (dvc, dvc_h), (dqp, dqp_h), (dk, dk_h), (dv, dv_h)])]
    stores += [pltpu.make_async_copy(dqc.at[pl.ds(t * 128, 128)], dqc_h.at[pl.ds(t * 128, 128)], os.at[5 + t]) for t in range(NB)]
    stores[0].start()
    stores[1].start()
    for t in range(5):
        n, rws = NKS[t], ROWS[t]
        r0 = t * 1024 if t < NB else RC
        for h in range(0, HEADS, 2):
            a, b = r0 + h * rws, r0 + (h + 2) * rws
            x = dot(DS[a:b, :n], kk[:n]) * RF[a:b, :]
            for j in range(2):
                y = x[j * rws:(j + 1) * rws].astype(BF)
                if t < NB:
                    dqc[t * 128:(t + 1) * 128, (h + j) * D:(h + j + 1) * D] = y
                else:
                    dqp[:, (h + j) * D:(h + j + 1) * D] = y
        stores[5 + t if t < NB else 2].start()

    tot = inc[pl.ds(chip, 1)][0].astype(F32) + part[shard(g), :].astype(F32)
    for j in range(1, CHIPS):
        s = lax.rem(chip + j, CHIPS)
        rc(summed.at[0], got.at[s], s2.at[0], r2.at[s], same[0]).wait_recv()
        tot = tot + got[pl.ds(s, 1)][0].astype(F32)
    dk[...] = tot[:, :D].astype(BF)
    dv[...] = tot[:, D:].astype(BF)
    stores[3].start()
    stores[4].start()
    for c in c1 + c2 + out + fwd + first:
        c.wait_send()
    for c in range(CHIPS):
        pl.when(chip != c)(second[c].wait_send)
    for c in stores:
        c.wait()


def backward(qc, kc, vc, dc, qp, pk, pv, dp, lengths, slot_of, passes):
    hbm = pl.BlockSpec(memory_space=pltpu.HBM)
    dma = lambda n: pltpu.SemaphoreType.DMA((n,))
    b = lambda *s: pltpu.VMEM(s, BF)
    f = lambda *s: pltpu.VMEM(s, F32)
    i = lambda *s: pltpu.VMEM(s, jnp.int32)
    o = lambda *s: jax.ShapeDtypeStruct(s, BF)
    return pl.pallas_call(
        backward_kernel,
        out_shape=(o(CR, 1024), o(CR, D), o(CR, D), o(PR, 1024), o(PR, D), o(PR, D)),
        in_specs=[hbm] * 11, out_specs=[hbm] * 6,
        scratch_shapes=[b(CR, 1024), b(CR, 1024), b(PR, 1024), b(PR, 1024), i(1, 16), i(1, 16), i(1, 4),
                        b(PK, 2 * D), b(CR, D), b(CR, D), b(NK, D), b(2 * D, NK), b(D, NK), b(RA, NK), b(RA, NK), b(D, RA), b(D, RA),
                        f(RA, D), b(HEADS * PR, D), b(HEADS * PR, D),
                        b(CR, 1024), b(PR, 1024), b(CR, D), b(CR, D), b(PR, D), b(PR, D), b(PK, 2 * D),
                        b(CHIPS, PR, 2 * D), b(CHIPS, PR, 2 * D), b(CHIPS, PR, 2 * D), f(8, D), f(NT - 1, 8, D), f(NG, 8, D)]
                       + [f(r, n) for r, n in zip(ROWS, NKS)] * 2
                       + [dma(11), dma(9), dma(2 * CHIPS - 1), dma(2 * CHIPS - 1), dma(NT - 1), dma(NT - 1), dma(NG - 1), dma(NG - 1),
                          dma(CHIPS), dma(CHIPS), dma(CHIPS), dma(CHIPS)],
        compiler_params=pltpu.CompilerParams(collective_id=1, has_side_effects=True, vmem_limit_bytes=63 << 20),
        name="attention_backward",
    )(qc, kc, vc, dc, qp, pk, pv, dp, lengths.reshape(1, 16), slot_of.reshape(1, 16), passes)


def result_kernel(*refs):
    n = (len(refs) - 1) // 2
    cs = [pltpu.make_async_copy(refs[i], refs[n + i], refs[-1].at[i]) for i in range(n)]
    for c in cs:
        c.start()
    for c in cs:
        c.wait()


def results(*xs):
    hbm = pl.BlockSpec(memory_space=pltpu.HBM)
    return pl.pallas_call(
        result_kernel, out_shape=tuple(jax.ShapeDtypeStruct(x.shape, x.dtype) for x in xs),
        in_specs=[hbm] * len(xs), out_specs=[hbm] * len(xs),
        scratch_shapes=[pltpu.SemaphoreType.DMA((len(xs),))], name="write_results",
    )(*xs)


def per_device(*args):
    return results(*backward(*args))


def solution(mesh):
    gt = P("group", "tensor")
    return jax.shard_map(per_device, mesh=mesh, in_specs=(gt,) * 8 + (P(), P(), gt), out_specs=(gt,) * 6, check_vma=False)
```

time: 330 us -> 103 us (0.31)
  Pallas kernels: 0 us -> 102 us
  blocking collectives: 100 us -> 0 us
  matrix products: 97.5 us -> 0 us
  waiting for transfers between devices: 55.4 us -> 0 us
  other arithmetic: 29.8 us -> 0 us
  local copies, waits for them, and re-layouts: 26.5 us -> 0 us
  between operations: 18.2 us -> 0.8 us
    pallas_call x0 -> x2, Pallas kernels: none -> 102 us  [the longest x1 53.9 us: backward(): pl.pallas_call(backward_kernel, out_shape=(o(CR, 1024), o(CR, D), o(CR, D...]
    dot_general x40 -> x0, matrix products: 97.5 us -> none  [the longest x8 39.7 us: head_terms(): jnp.einsum('rhk,rhd->khd', weights_b, cot_head, preferred_element_type=jn...]
    psum x2 -> x0, blocking collectives: 55.5 us -> none  [the longest x1 37 us: per_device(): rewards = lax.psum(table, 'group')]
    reduce_scatter x1 -> x0, waiting for transfers between devices: 55.4 us -> none  [per_device(): lax.psum_scatter(key_grads[:prompt_len], 'group', scatter_dimension=0, ti...]
    all_gather x2 -> x0, blocking collectives: 44.8 us -> none  [the longest x1 23.5 us: per_device(): lax.all_gather(prompt_value_array, 'group', axis=0, tiled=True)]
    while x98 -> x0, local copies, waits for them, and re-layouts: 18.4 us -> none
    another operation x9 -> x0, other arithmetic: 12.8 us -> none
    reduce_sum x12 -> x0, other arithmetic: 10.3 us -> none  [the longest x8 6.48 us: head_terms(): row_total = jnp.sum(exps, axis=2, keepdims=True)]
  transfers between devices with their start and end apart: 1 -> 0, of which waited for: 1 -> 0; matrix products, arithmetic and copies ran while one was open for 1% -> 0% of each run, Pallas kernels for 0% -> 0%
where the time goes in v2:
time: 103 us
  Pallas kernels  102 us (99%)
    pallas_call x1, Pallas kernels, backward(): pl.pallas_call(backward_kernel, out_shape=(o(CR, 1024), o(CR, D), o(CR, D...  53.9 us
    pallas_call x1, Pallas kernels, results(): pl.pallas_call(result_kernel, out_shape=tuple((jax.ShapeDtypeStruct(x.sha...  48.3 us

profile of v2, /device:TPU:1, one launch (start us, length us, event | category | flops | bytes accessed | tf_op | source)
XLA Modules:
  0.0 103.0 jit_solution(1298913518929882453)
XLA Ops:
  0.6 53.9 %attention_backward.1 = (bf16[512,1024]{1,0:T(8,128)(2,1)}, bf16[512,128]{1,0:T(8,128)(2,1)}, bf16[512,128]{1,0:T(8,128)(2,1)}, bf16[96,1024]{1,0:T(8,128)(2,1)}...) custom-call(bf16[512,1024]{1,0:T(8,128)(2,1)} %qc_h.1, bf16[512,128]{1,0:T(8,128)(2,1)} %kc_h.1, ...), custom_call_target="tpu_custom_call" | custom-call | tf_op jit(solution)/shard_map/attention_backward/pallas_call | solution.py:264
  54.5 48.3 %write_results.1 = (bf16[512,1024]{1,0:T(8,128)(2,1)}, bf16[512,128]{1,0:T(8,128)(2,1)}, bf16[512,128]{1,0:T(8,128)(2,1)}, bf16[96,1024]{1,0:T(8,128)(2,1)}, bf1...) custom-call(bf16[512,1024]{1,0:T(8,128)(2,1)} %get-tuple-element.12.refs_0_, bf16[512,128]{1,0:T(8,128)(2,1)} %get-tuple-element.13.refs_1_, ...), custom_call_target="tpu_custom_call" | custom-call | tf_op jit(solution)/shard_map/write_results/pallas_call | solution.py:292

commit v3 on v2

--- a/solution.py
+++ b/solution.py
@@ -279,20 +279,28 @@
 
 
 def result_kernel(*refs):
-    n = (len(refs) - 1) // 2
-    cs = [pltpu.make_async_copy(refs[i], refs[n + i], refs[-1].at[i]) for i in range(n)]
-    for c in cs:
+    n = len(refs) // 3
+    src, dst, buf, (ls, os) = refs[:n], refs[n:2 * n], refs[2 * n:3 * n], refs[3 * n:]
+    cuts = [(i, r) for i in range(n) for r in range(0, src[i].shape[0], 128)]
+    at = lambda ref, r: ref.at[pl.ds(r, min(128, ref.shape[0] - r))]
+    a = [pltpu.make_async_copy(at(src[i], r), at(buf[i], r), ls.at[k]) for k, (i, r) in enumerate(cuts)]
+    b = [pltpu.make_async_copy(at(buf[i], r), at(dst[i], r), os.at[k]) for k, (i, r) in enumerate(cuts)]
+    for c in a:
         c.start()
-    for c in cs:
+    for c, d in zip(a, b):
+        c.wait()
+        d.start()
+    for c in b:
         c.wait()
 
 
 def results(*xs):
     hbm = pl.BlockSpec(memory_space=pltpu.HBM)
+    n = sum(-(-x.shape[0] // 128) for x in xs)
     return pl.pallas_call(
         result_kernel, out_shape=tuple(jax.ShapeDtypeStruct(x.shape, x.dtype) for x in xs),
         in_specs=[hbm] * len(xs), out_specs=[hbm] * len(xs),
-        scratch_shapes=[pltpu.SemaphoreType.DMA((len(xs),))], name="write_results",
+        scratch_shapes=[pltpu.VMEM(x.shape, x.dtype) for x in xs] + [pltpu.SemaphoreType.DMA((n,))] * 2, name="write_results",
     )(*xs)
 
 

time: 103 us -> 57.2 us (0.56)
  Pallas kernels: 102 us -> 56.2 us
    pallas_call x1, Pallas kernels: 48.3 us -> 2.33 us  [results(): pl.pallas_call(result_kernel, out_shape=tuple((jax.ShapeDtypeStruct(x.sha...]
where the time goes in v3:
time: 57.2 us; the launch traced here: 57 us
  Pallas kernels  56.2 us (98%)
  between operations  0.8 us (1%)
    pallas_call x1, Pallas kernels, backward(): pl.pallas_call(backward_kernel, out_shape=(o(CR, 1024), o(CR, D), o(CR, D...  53.9 us
    pallas_call x1, Pallas kernels, results(): pl.pallas_call(result_kernel, out_shape=tuple((jax.ShapeDtypeStruct(x.sha...  2.33 us

profile of v3, /device:TPU:1, one launch (start us, length us, event | category | flops | bytes accessed | tf_op | source)
XLA Modules:
  0.0 57.0 jit_solution(3662241838255948848)
XLA Ops:
  0.6 53.9 %attention_backward.1 = (bf16[512,1024]{1,0:T(8,128)(2,1)}, bf16[512,128]{1,0:T(8,128)(2,1)}, bf16[512,128]{1,0:T(8,128)(2,1)}, bf16[96,1024]{1,0:T(8,128)(2,1)}...) custom-call(bf16[512,1024]{1,0:T(8,128)(2,1)} %qc_h.1, bf16[512,128]{1,0:T(8,128)(2,1)} %kc_h.1, ...), custom_call_target="tpu_custom_call" | custom-call | tf_op jit(solution)/shard_map/attention_backward/pallas_call | solution.py:264
  54.5 2.3 %write_results.1 = (bf16[512,1024]{1,0:T(8,128)(2,1)}, bf16[512,128]{1,0:T(8,128)(2,1)}, bf16[512,128]{1,0:T(8,128)(2,1)}, bf16[96,1024]{1,0:T(8,128)(2,1)}, bf1...) custom-call(bf16[512,1024]{1,0:T(8,128)(2,1)} %get-tuple-element.12.refs_0_, bf16[512,128]{1,0:T(8,128)(2,1)} %get-tuple-element.13.refs_1_, ...), custom_call_target="tpu_custom_call" | custom-call | tf_op jit(solution)/shard_map/write_results/pallas_call | solution.py:300

commit v4 on v3

v4 whole, which is shorter than its diff:
```python
import jax
import jax.numpy as jnp
from jax import lax
from jax.experimental import pallas as pl
from jax.experimental.pallas import tpu as pltpu
from jax.sharding import PartitionSpec as P

MESH = pl.DeviceIdType.MESH
NG, NT, TESTS, MAXB, BLK = 16, 8, 32, 4, 128
F32, BF = jnp.float32, jnp.bfloat16
HEADS, D, CR, PR, PK = 8, 128, 512, 96, 1536
NB = CR // 128
NK = PK + CR
RC = HEADS * CR
RA = RC + HEADS * PR
SCALE = D ** -0.5
C2 = SCALE * 1.4426950408889634
NKS = [PK + 128 * (i + 1) for i in range(NB)] + [PK]
RP = HEADS * PR
GC = 256
KB = 32
KEYS = 384
CHIPS = NG // 2


def dot_t(a, b):
    return lax.dot_general(a, b, (((1,), (1,)), ((), ())), preferred_element_type=F32)


def dot(a, b):
    return lax.dot_general(a, b, (((1,), (0,)), ((), ())), preferred_element_type=F32)


def backward_kernel(qc_h, kc_h, vc_h, dc_h, qp_h, pk_h, pv_h, dp_h, len_h, slot_h, passes_h,
                    dqc_h, dkc_h, dvc_h, dqp_h, dk_h, dv_h,
                    qc, dc, qp, dp, lens, slots, passes, kv, kc, vc, kk, vv, W, DS, QR, OR, RF, qps, dps, dqs, pos,
                    dqc, dqp, dkc, dvc, dk, dv, part, inc, summed, got, cnt, cnt_in, rew,
                    S0, S1, T0, T1,
                    ls, os, gs, gr, cs, cr, ws, wr, s1, r1, s2, r2):
    S, T = [S0, S1], [T0, T1]
    g, t_ax = lax.axis_index("group"), lax.axis_index("tensor")
    chip, core = g // 2, lax.rem(g, 2)
    same = [(2 * lax.rem(chip + j, CHIPS) + core, t_ax) for j in range(1, CHIPS)]
    sib = (2 * chip + 1 - core, t_ax)
    group = [(lax.rem(g + j, NG), t_ax) for j in range(1, NG)]
    tens = [(g, lax.rem(t_ax + j, NT)) for j in range(1, NT)]

    def rc(src, dst, s, r, d):
        return pltpu.make_async_remote_copy(src_ref=src, dst_ref=dst, send_sem=s, recv_sem=r, device_id=d, device_id_type=MESH)

    def shard(s):
        return pl.ds(pl.multiple_of(s * PR, 32), PR)

    barrier = pltpu.get_barrier_semaphore()
    for d in group + tens:
        pl.semaphore_signal(barrier, inc=1, device_id=d, device_id_type=MESH)
    mine = shard(g)
    loads = [pltpu.make_async_copy(a, b, ls.at[i]) for i, (a, b) in enumerate([
        (pk_h, kv.at[mine, pl.ds(0, D)]), (pv_h, kv.at[mine, pl.ds(D, D)]), (passes_h, passes), (kc_h, kc), (vc_h, vc),
        (len_h, lens), (slot_h, slots), (qc_h, qc), (dc_h, dc), (qp_h, qp), (dp_h, dp)])]
    for c in loads:
        c.start()
    for c in loads[:3]:
        c.wait()
    cnt[...] = jnp.broadcast_to(jnp.sum(passes[...].astype(F32), axis=1, keepdims=True), (8, D))
    pl.semaphore_wait(barrier, len(group) + len(tens))

    c1 = [rc(cnt, cnt_in.at[j], cs.at[j], cr.at[j], tens[j]) for j in range(NT - 1)]
    out = [rc(kv.at[mine], kv.at[mine], gs.at[j], gr.at[j], same[j - 1] if j else sib) for j in range(CHIPS)]
    for c in out + c1:
        c.start()
    for c in loads[3:]:
        c.wait()
    kk[PK:] = kc[...]
    vv[PK:] = vc[...]
    for h in range(HEADS):
        qps[h * PR:(h + 1) * PR] = qp[:, h * D:(h + 1) * D]
        dps[h * PR:(h + 1) * PR] = dp[:, h * D:(h + 1) * D]
    pos[...] = lax.rem(lax.broadcasted_iota(jnp.int32, (8, RP), 1), PR) + g * PR
    for c in c1:
        c.wait_recv()
    total = cnt[...]
    for j in range(NT - 1):
        total = total + cnt_in[j]
    rew[pl.ds(g, 1)] = (total / TESTS)[None]
    c2 = [rc(rew.at[pl.ds(g, 1)], rew.at[pl.ds(g, 1)], ws.at[j], wr.at[j], group[j]) for j in range(NG - 1)]
    for c in c2:
        c.start()
    fwd = []
    for j in range(1, CHIPS):
        out[j].wait_recv()
        rows = shard(2 * lax.rem(chip - j + CHIPS, CHIPS) + core)
        f = rc(kv.at[rows], kv.at[rows], gs.at[CHIPS - 1 + j], gr.at[CHIPS - 1 + j], sib)
        f.start()
        fwd.append(f)
    out[0].wait_recv()
    for f in fwd:
        f.wait_recv()
    kk[:PK] = kv[:, :D]
    vv[:PK] = kv[:, D:]

    def cols(h):
        return pl.ds(pl.multiple_of(h * D, D), D)

    def group_cols(t, p):
        return pl.ds(pl.multiple_of(t * 1024 + p * GC, GC), GC)

    def qo(t, p):
        if t == NB:
            return qps[p * GC:(p + 1) * GC], dps[p * GC:(p + 1) * GC]
        sl = slice(t * 128, (t + 1) * 128)
        a, b = cols(2 * p), cols(2 * p + 1)
        return jnp.concatenate([qc[sl, a], qc[sl, b]], axis=0), jnp.concatenate([dc[sl, a], dc[sl, b]], axis=0)

    zs = lambda u: u // 8
    zl = lambda u: (u + 1) // 9

    def products(t, p, u, slot):
        n = NKS[t]
        q, o = qo(t, p)
        xs = q.astype(F32) * C2
        hi = xs.astype(BF)
        ql = jnp.concatenate([hi, (xs - hi.astype(F32)).astype(BF)], axis=1)

        def piece(a, b):
            ka = kk[a:b]
            s = dot_t(jnp.concatenate([ka, ka], axis=1), ql)
            if t == NB:
                k = lax.broadcasted_iota(jnp.int32, s.shape, 0) + a
                s = jnp.where(k <= pos[:1, p * GC:(p + 1) * GC], s, -1e30)
            elif b == n:
                k = lax.broadcasted_iota(jnp.int32, (128, GC), 0)
                r = lax.rem(lax.broadcasted_iota(jnp.int32, (128, GC), 1), 128)
                s = jnp.concatenate([s[:b - a - 128], jnp.where(k <= r, s[b - a - 128:], -1e30)], axis=0)
            S[slot][zs(u), a:b] = s
            T[slot][zs(u), a:b] = dot_t(vv[a:b], o)
        cut = [n * i // 3 // 128 * 128 for i in range(3)] + [n]
        return [lambda a=a, b=b: piece(a, b) for a, b in zip(cut[:-1], cut[1:])]

    def softmax(t, p, u, slot):
        n = NKS[t]
        cs = group_cols(t, p) if t < NB else pl.ds(RC + p * GC, GC)
        z = zl(u)
        st = {}

        def top():
            st["m"] = jnp.max(S[slot][z, :n], axis=0, keepdims=True)

        def weights():
            tot = dr = None
            for k in range(0, n, KB):
                e = jnp.exp2(S[slot][z, k:k + KB] - st["m"])
                x = e * T[slot][z, k:k + KB]
                W[k:k + KB, cs] = e.astype(BF)
                a = jnp.sum(e.reshape(KB // 8, 8, GC), axis=0)
                b = jnp.sum(x.reshape(KB // 8, 8, GC), axis=0)
                tot = a if tot is None else tot + a
                dr = b if dr is None else dr + b
            r = 1.0 / jnp.sum(tot, axis=0, keepdims=True)
            st["d"] = jnp.sum(dr, axis=0, keepdims=True) * r
            if t < NB:
                row = lax.rem(lax.broadcasted_iota(jnp.int32, (1, GC), 1), 128) + t * 128
                r = r * jnp.where(row.astype(F32) < live, fac, 0.0)
            RF[:, cs] = jnp.broadcast_to(r * SCALE, (8, GC))
            st["r"] = r

        def grads():
            for k in range(0, n, KB):
                DS[k:k + KB, cs] = (W[k:k + KB, cs].astype(F32) * (T[slot][z, k:k + KB] - st["d"])).astype(BF)
            rt = jnp.transpose(jnp.broadcast_to(st["r"], (D, GC)))
            q, o = qo(t, p)
            QR[cs, :] = (q.astype(F32) * (rt * SCALE)).astype(BF)
            OR[cs, :] = (o.astype(F32) * rt).astype(BF)
        return [top, weights, grads]

    def step(nxt, cur, u, slot):
        a = products(*nxt, u, 1 - slot) if nxt else [lambda: None] * 3
        for f, h in zip(a, softmax(*cur, u, slot)):
            f()
            h()

    for f in products(0, 0, core // 2, 0):
        f()
    for c in c2:
        c.wait_recv()
    center = rew[0]
    for s in range(1, NG):
        center = center + rew[s]
    blocks = jnp.sum(jnp.where(slots[...] == g, lens[...], 0).astype(F32), axis=1, keepdims=True)
    adv = rew[pl.ds(g, 1)][0][:1, :1] - (center / NG)[:1, :1]
    fac = adv * MAXB / blocks
    live = blocks * BLK

    @pl.loop(0, HEADS // 2)
    def _(p):
        for t in range(NB):
            step((t + 1, p) if t < NB - 1 else (0, lax.rem(p + 1, HEADS // 2)), (t, p), p, t % 2)
    for f in products(NB, 0, core // 2, 0):
        f()
    for p in range(RP // GC):
        step((NB, p + 1) if p + 1 < RP // GC else None, (NB, p), core // 2, p % 2)

    def key_block(b):
        lo, hi = b * KEYS, (b + 1) * KEYS
        part[lo:hi, :D] = dot(DS[lo:hi], QR[...]).astype(BF)
        part[lo:hi, D:] = dot(W[lo:hi], OR[...]).astype(BF)

    first = [rc(part.at[shard(2 * c + 1 - core)], inc.at[c], s1.at[c], r1.at[c], sib) for c in range(CHIPS)]
    second = [rc(summed.at[c], got.at[chip], s2.at[c], r2.at[chip], (2 * c + core, t_ax)) for c in range(CHIPS)]

    def pass_on(c):
        first[c].wait_recv()
        x = inc[c].astype(F32) + part[shard(2 * c + core), :].astype(F32)
        summed[c] = x.astype(BF)
        pl.when(chip != c)(second[c].start)

    per = KEYS // (2 * PR)
    for b in range(PK // KEYS):
        key_block(b)
        for c in range(b * per, (b + 1) * per):
            first[c].start()
        for c in range((b - 1) * per, b * per) if b else ():
            pass_on(c)
    for i in range(NB):
        sl = slice(i * 128, (i + 1) * 128)
        rows, cs = slice(PK + i * 128, PK + (i + 1) * 128), slice(i * 1024, RC)
        dkc[sl] = dot(DS[rows, cs], QR[cs]).astype(BF)
        dvc[sl] = dot(W[rows, cs], OR[cs]).astype(BF)
    for c in range(CHIPS - per, CHIPS):
        pass_on(c)

    stores = [pltpu.make_async_copy(a, b, os.at[i]) for i, (a, b) in enumerate([
        (dkc, dkc_h), (dvc, dvc_h), (dqp, dqp_h), (dk, dk_h), (dv, dv_h)])]
    stores += [pltpu.make_async_copy(dqc.at[pl.ds(t * 128, 128)], dqc_h.at[pl.ds(t * 128, 128)], os.at[5 + t]) for t in range(NB)]
    stores[0].start()
    stores[1].start()
    kt = jnp.transpose(kk[...])
    for t in range(NB + 1):
        n = NKS[t]
        for c in range(0, 1024 if t < NB else RP, GC):
            a = t * 1024 + c
            x = jnp.transpose(dot(kt[:, :n], DS[:n, a:a + GC]) * RF[:1, a:a + GC]).astype(BF)
            if t < NB:
                for j in range(2):
                    dqc[t * 128:(t + 1) * 128, c + j * D:c + (j + 1) * D] = x[j * 128:(j + 1) * 128]
            else:
                dqs[c:c + GC] = x
        if t < NB:
            stores[5 + t].start()
    for h in range(HEADS):
        dqp[:, h * D:(h + 1) * D] = dqs[h * PR:(h + 1) * PR]
    stores[2].start()

    tot = inc[pl.ds(chip, 1)][0].astype(F32) + part[shard(g), :].astype(F32)
    for j in range(1, CHIPS):
        s = lax.rem(chip + j, CHIPS)
        rc(summed.at[0], got.at[s], s2.at[0], r2.at[s], same[0]).wait_recv()
        tot = tot + got[pl.ds(s, 1)][0].astype(F32)
    dk[...] = tot[:, :D].astype(BF)
    dv[...] = tot[:, D:].astype(BF)
    stores[3].start()
    stores[4].start()
    for c in c1 + c2 + out + fwd + first:
        c.wait_send()
    for c in range(CHIPS):
        pl.when(chip != c)(second[c].wait_send)
    for c in stores:
        c.wait()


def backward(qc, kc, vc, dc, qp, pk, pv, dp, lengths, slot_of, passes):
    hbm = pl.BlockSpec(memory_space=pltpu.HBM)
    dma = lambda n: pltpu.SemaphoreType.DMA((n,))
    b = lambda *s: pltpu.VMEM(s, BF)
    f = lambda *s: pltpu.VMEM(s, F32)
    i = lambda *s: pltpu.VMEM(s, jnp.int32)
    o = lambda *s: jax.ShapeDtypeStruct(s, BF)
    return pl.pallas_call(
        backward_kernel,
        out_shape=(o(CR, 1024), o(CR, D), o(CR, D), o(PR, 1024), o(PR, D), o(PR, D)),
        in_specs=[hbm] * 11, out_specs=[hbm] * 6,
        scratch_shapes=[b(CR, 1024), b(CR, 1024), b(PR, 1024), b(PR, 1024), i(1, 16), i(1, 16), i(1, 4),
                        b(PK, 2 * D), b(CR, D), b(CR, D), b(NK, D), b(NK, D), b(NK, RA), b(NK, RA), b(RA, D), b(RA, D),
                        f(8, RA), b(RP, D), b(RP, D), b(RP, D), i(8, RP),
                        b(CR, 1024), b(PR, 1024), b(CR, D), b(CR, D), b(PR, D), b(PR, D), b(PK, 2 * D),
                        b(CHIPS, PR, 2 * D), b(CHIPS, PR, 2 * D), b(CHIPS, PR, 2 * D), f(8, D), f(NT - 1, 8, D), f(NG, 8, D)]
                       + [f(1, NK, GC)] * 4
                       + [dma(11), dma(9), dma(2 * CHIPS - 1), dma(2 * CHIPS - 1), dma(NT - 1), dma(NT - 1), dma(NG - 1), dma(NG - 1),
                          dma(CHIPS), dma(CHIPS), dma(CHIPS), dma(CHIPS)],
        compiler_params=pltpu.CompilerParams(collective_id=1, has_side_effects=True, vmem_limit_bytes=63 << 20),
        name="attention_backward",
    )(qc, kc, vc, dc, qp, pk, pv, dp, lengths.reshape(1, 16), slot_of.reshape(1, 16), passes)


def result_kernel(*refs):
    n = len(refs) // 3
    src, dst, buf, (ls, os) = refs[:n], refs[n:2 * n], refs[2 * n:3 * n], refs[3 * n:]
    cuts = [(i, r) for i in range(n) for r in range(0, src[i].shape[0], 128)]
    at = lambda ref, r: ref.at[pl.ds(r, min(128, ref.shape[0] - r))]
    a = [pltpu.make_async_copy(at(src[i], r), at(buf[i], r), ls.at[k]) for k, (i, r) in enumerate(cuts)]
    b = [pltpu.make_async_copy(at(buf[i], r), at(dst[i], r), os.at[k]) for k, (i, r) in enumerate(cuts)]
    for c in a:
        c.start()
    for c, d in zip(a, b):
        c.wait()
        d.start()
    for c in b:
        c.wait()


def results(*xs):
    hbm = pl.BlockSpec(memory_space=pltpu.HBM)
    n = sum(-(-x.shape[0] // 128) for x in xs)
    return pl.pallas_call(
        result_kernel, out_shape=tuple(jax.ShapeDtypeStruct(x.shape, x.dtype) for x in xs),
        in_specs=[hbm] * len(xs), out_specs=[hbm] * len(xs),
        scratch_shapes=[pltpu.VMEM(x.shape, x.dtype) for x in xs] + [pltpu.SemaphoreType.DMA((n,))] * 2, name="write_results",
    )(*xs)


def per_device(*args):
    return results(*backward(*args))


def solution(mesh):
    gt = P("group", "tensor")
    return jax.shard_map(per_device, mesh=mesh, in_specs=(gt,) * 8 + (P(), P(), gt), out_specs=(gt,) * 6, check_vma=False)
```

time: 57.2 us -> 62.7 us (1.096)
  the two profiles are of different devices: /device:TPU:1 before, /device:TPU:7 now
where the time goes in v4:
time: 62.7 us; the launch traced here: 62.6 us
  Pallas kernels  61.7 us (98%)
  between operations  0.8 us (1%)
    pallas_call x1, Pallas kernels, backward(): pl.pallas_call(backward_kernel, out_shape=(o(CR, 1024), o(CR, D), o(CR, D...  59.4 us
    pallas_call x1, Pallas kernels, results(): pl.pallas_call(result_kernel, out_shape=tuple((jax.ShapeDtypeStruct(x.sha...  2.33 us

profile of v4, /device:TPU:7, one launch (start us, length us, event | category | flops | bytes accessed | tf_op | source)
XLA Modules:
  0.0 62.6 jit_solution(2172177822973022815)
XLA Ops:
  0.6 59.4 %attention_backward.1 = (bf16[512,1024]{1,0:T(8,128)(2,1)}, bf16[512,128]{1,0:T(8,128)(2,1)}, bf16[512,128]{1,0:T(8,128)(2,1)}, bf16[96,1024]{1,0:T(8,128)(2,1)}...) custom-call(bf16[512,1024]{1,0:T(8,128)(2,1)} %qc_h.1, bf16[512,128]{1,0:T(8,128)(2,1)} %kc_h.1, ...), custom_call_target="tpu_custom_call" | custom-call | tf_op jit(solution)/shard_map/attention_backward/pallas_call | solution.py:278
  60.1 2.3 %write_results.1 = (bf16[512,1024]{1,0:T(8,128)(2,1)}, bf16[512,128]{1,0:T(8,128)(2,1)}, bf16[512,128]{1,0:T(8,128)(2,1)}, bf16[96,1024]{1,0:T(8,128)(2,1)}, bf1...) custom-call(bf16[512,1024]{1,0:T(8,128)(2,1)} %get-tuple-element.12.refs_0_, bf16[512,128]{1,0:T(8,128)(2,1)} %get-tuple-element.13.refs_1_, ...), custom_call_target="tpu_custom_call" | custom-call | tf_op jit(solution)/shard_map/write_results/pallas_call | solution.py:314

commit v5 on v3

--- a/solution.py
+++ b/solution.py
@@ -57,20 +57,22 @@
         z = jnp.zeros((1024, 128), BF)
         W[i * 1024:(i + 1) * 1024, PK + (i + 1) * 128:PK + (i + 2) * 128] = z
         DS[i * 1024:(i + 1) * 1024, PK + (i + 1) * 128:PK + (i + 2) * 128] = z
-    for c in loads:
+    for c in loads[:3]:
         c.wait()
     cnt[...] = jnp.broadcast_to(jnp.sum(passes[...].astype(F32), axis=1, keepdims=True), (8, D))
+    pl.semaphore_wait(barrier, len(group) + len(tens))
+
+    c1 = [rc(cnt, cnt_in.at[j], cs.at[j], cr.at[j], tens[j]) for j in range(NT - 1)]
+    out = [rc(kv.at[mine], kv.at[mine], gs.at[j], gr.at[j], same[j - 1] if j else sib) for j in range(CHIPS)]
+    for c in out + c1:
+        c.start()
+    for c in loads[3:]:
+        c.wait()
     kk[PK:] = kc[...]
     kt = jnp.transpose(kc[...])
     kkt[:D, PK:] = kt
     kkt[D:, PK:] = kt
     vt[:, PK:] = jnp.transpose(vc[...])
-    pl.semaphore_wait(barrier, len(group) + len(tens))
-
-    c1 = [rc(cnt, cnt_in.at[j], cs.at[j], cr.at[j], tens[j]) for j in range(NT - 1)]
-    out = [rc(kv.at[mine], kv.at[mine], gs.at[j], gr.at[j], same[j - 1] if j else sib) for j in range(CHIPS)]
-    for c in c1 + out:
-        c.start()
     for c in c1:
         c.wait_recv()
     total = cnt[...]
@@ -130,14 +132,7 @@
         T[t][...] = dot(o, vt[:, :n])
 
     products(0, 0)
-    for c in c2:
-        c.wait_recv()
-    center = rew[0]
-    for s in range(1, NG):
-        center = center + rew[s]
     blocks = jnp.sum(jnp.where(slots[...] == g, lens[...], 0).astype(F32), axis=1, keepdims=True)
-    adv = rew[pl.ds(g, 1)][0][:1] - (center / NG)[:1]
-    fac = adv * MAXB / blocks
     live = blocks * BLK
 
     def softmax(t, h):
@@ -155,7 +150,7 @@
         DS[out, :n] = (e * (d - drift)).astype(BF)
         if t < NB:
             row = lax.broadcasted_iota(jnp.int32, (128, D), 0) + t * 128
-            r = r * jnp.where(row.astype(F32) < live, fac, 0.0)
+            r = r * jnp.where(row.astype(F32) < live, 1.0, 0.0)
         else:
             r = jnp.broadcast_to(r, (PR, D))
         RF[out, :] = r * SCALE
@@ -182,11 +177,24 @@
     QT[:, RC:] = jnp.transpose(QP[...])
     OT[:, RC:] = jnp.transpose(OP[...])
 
+    for c in c2:
+        c.wait_recv()
+    center = rew[0]
+    for s in range(1, NG):
+        center = center + rew[s]
+    adv = rew[pl.ds(g, 1)][0][:1] - (center / NG)[:1]
+    fac = adv * MAXB / blocks
+
     def key_block(b):
         lo, hi = b * 256, (b + 1) * 256
-        r0, r1_ = (0, RA) if lo < PK else (((lo - PK) // 128) * 1024, RC)
-        gv = jnp.transpose(dot(OT[:, r0:r1_], W[r0:r1_, lo:hi])).astype(BF)
-        gk = jnp.transpose(dot(QT[:, r0:r1_], DS[r0:r1_, lo:hi])).astype(BF)
+        r0 = 0 if lo < PK else ((lo - PK) // 128) * 1024
+        f = jnp.concatenate([fac, fac], axis=1)
+        gv = dot(OT[:, r0:RC], W[r0:RC, lo:hi]) * f
+        gk = dot(QT[:, r0:RC], DS[r0:RC, lo:hi]) * f
+        if lo < PK:
+            gv = gv + dot(OT[:, RC:], W[RC:, lo:hi])
+            gk = gk + dot(QT[:, RC:], DS[RC:, lo:hi])
+        gv, gk = jnp.transpose(gv).astype(BF), jnp.transpose(gk).astype(BF)
         if lo < PK:
             part[lo:hi, :D] = gk
             part[lo:hi, D:] = gv
@@ -228,7 +236,7 @@
         r0 = t * 1024 if t < NB else RC
         for h in range(0, HEADS, 2):
             a, b = r0 + h * rws, r0 + (h + 2) * rws
-            x = dot(DS[a:b, :n], kk[:n]) * RF[a:b, :]
+            x = dot(DS[a:b, :n], kk[:n]) * (RF[a:b, :] * fac if t < NB else RF[a:b, :])
             for j in range(2):
                 y = x[j * rws:(j + 1) * rws].astype(BF)
                 if t < NB:

time: 57.2 us -> 57.7 us (level); the launches traced: 57 us -> 56.5 us
  no operation moved by 1% of the time
where the time goes in v5:
time: 57.7 us; the launch traced here: 56.5 us
  Pallas kernels  55.7 us (97%)
  between operations  0.8 us (1%)
    pallas_call x1, Pallas kernels, backward(): pl.pallas_call(backward_kernel, out_shape=(o(CR, 1024), o(CR, D), o(CR, D...  53.4 us
    pallas_call x1, Pallas kernels, results(): pl.pallas_call(result_kernel, out_shape=tuple((jax.ShapeDtypeStruct(x.sha...  2.33 us

profile of v5, /device:TPU:1, one launch (start us, length us, event | category | flops | bytes accessed | tf_op | source)
XLA Modules:
  0.0 56.5 jit_solution(7276942192142502011)
XLA Ops:
  0.6 53.4 %attention_backward.1 = (bf16[512,1024]{1,0:T(8,128)(2,1)}, bf16[512,128]{1,0:T(8,128)(2,1)}, bf16[512,128]{1,0:T(8,128)(2,1)}, bf16[96,1024]{1,0:T(8,128)(2,1)}...) custom-call(bf16[512,1024]{1,0:T(8,128)(2,1)} %qc_h.1, bf16[512,128]{1,0:T(8,128)(2,1)} %kc_h.1, ...), custom_call_target="tpu_custom_call" | custom-call | tf_op jit(solution)/shard_map/attention_backward/pallas_call | solution.py:272
  54.1 2.3 %write_results.1 = (bf16[512,1024]{1,0:T(8,128)(2,1)}, bf16[512,128]{1,0:T(8,128)(2,1)}, bf16[512,128]{1,0:T(8,128)(2,1)}, bf16[96,1024]{1,0:T(8,128)(2,1)}, bf1...) custom-call(bf16[512,1024]{1,0:T(8,128)(2,1)} %get-tuple-element.12.refs_0_, bf16[512,128]{1,0:T(8,128)(2,1)} %get-tuple-element.13.refs_1_, ...), custom_call_target="tpu_custom_call" | custom-call | tf_op jit(solution)/shard_map/write_results/pallas_call | solution.py:308
